TPU v7x, 128 devices: a whole 4x4x4 slice. The times are simulated.
128 devices in a mesh: seq: 16 (over x, y_lo, core), tp: 8 (over y_hi, z).
Axes of the slice: x: 4, y: 4 (y_hi: 2, y_lo: 2; y = y_hi * 2 + y_lo), z: 4, core: 2. Of those that a mesh axis runs over, the one named last changes fastest.
Arguments:
- query_proj: bfloat16 [2560, 4096], P('seq', 'tp'), may hold values from -6 to 6
- key_proj: bfloat16 [2560, 4096], P('seq', 'tp'), may hold values from -6 to 6
- value_proj: bfloat16 [2560, 4096], P('seq', 'tp'), may hold values from -6 to 6
- query_tan: bfloat16 [2560, 4096], P('seq', 'tp'), may hold values from -6 to 6
- key_tan: bfloat16 [2560, 4096], P('seq', 'tp'), may hold values from -6 to 6
- value_tan: bfloat16 [2560, 4096], P('seq', 'tp'), may hold values from -6 to 6
- out_weight: bfloat16 [4096, 4096], P('tp'), may hold values from -0.09375 to 0.09375
- noisy_latent: bfloat16 [2560, 4096], P(('seq', 'tp')), may hold values from -20 to 20
- latent_velocity: bfloat16 [2560, 4096], P(('seq', 'tp')), may hold values from -20 to 20
- time_index: int32 [16], replicated, may hold values from 0 to 63
- frame_lengths: int32 [16], replicated, may hold values from 1 to 320, 2560 in all
Outputs:
- grad_query: bfloat16 [2560, 4096], P('seq', 'tp')
- grad_key: bfloat16 [2560, 4096], P('seq', 'tp')
- grad_value: bfloat16 [2560, 4096], P('seq', 'tp')
- grad_out_proj: bfloat16 [4096, 4096], P('tp', 'seq')
All inputs are finite; a program needn't handle non-finite values.
Results may differ from a plain program's by a relative error of at most 0.025.
Values may be sent and summed in bfloat16 or wider, within the bound.
A program may use at most 64 MiB of HBM per device.

v0:
```python
import math

import jax
import jax.numpy as jnp
from jax import lax
from jax.sharding import PartitionSpec as P

HEAD_DIM = 128
TSTEPS = 64


neg_large = -1e30


def shifted(value, axis, by):
    count = lax.axis_size(axis)
    return lax.ppermute(value, axis, [(i, (i + by) % count) for i in range(count)])


def frame_of(positions, frame_ends):
    return jnp.sum((positions[:, None] >= frame_ends[None, :]).astype(jnp.int32), axis=1)


def split_rows(total_rows):
    block_rows = total_rows
    while block_rows > 1024 and block_rows % 2 == 0:
        block_rows = block_rows // 2
    return block_rows


def over_blocks(carry, arrays, step_fn):
    total_rows = arrays[0].shape[0]
    block_rows = split_rows(total_rows)
    block_count = total_rows // block_rows

    def loop_step(block_number, state):
        offset = block_number * block_rows
        pieces = tuple(
            (lax.dynamic_slice_in_dim(member, offset, block_rows, 0) for member in arrays)
        )
        return step_fn(state, pieces, offset)

    return lax.fori_loop(0, block_count, loop_step, carry)


def on_device(
    query_proj,
    key_proj,
    value_proj,
    query_tan,
    key_tan,
    value_tan,
    out_weight,
    noisy_latent,
    latent_velocity,
    time_index,
    frame_lengths,
):
    local_rows, local_width = query_proj.shape
    head_count = local_width // HEAD_DIM
    scale = 1.0 / math.sqrt(HEAD_DIM)
    highest = lax.Precision.HIGHEST
    frame_ends = jnp.cumsum(frame_lengths)
    seq_index = lax.axis_index("seq")
    cycle_length = lax.axis_size("seq")
    row_offsets = jnp.arange(local_rows, dtype=jnp.int32)
    own_frames = frame_of(seq_index * local_rows + row_offsets, frame_ends)

    def heads(array):
        return array.reshape(array.shape[0], head_count, HEAD_DIM)

    def flat(array):
        return array.reshape(array.shape[0], local_width)

    queries = heads(query_proj)
    queries_dot = heads(query_tan)

    def forward_step(state, pieces, first_row):
        run_max, run_total, run_tan, acc_out, acc_tan = state
        keys_block, values_block, keys_dot, values_dot = [heads(member) for member in pieces]
        values_wide = values_block.astype(jnp.float32)
        values_dot_wide = values_dot.astype(jnp.float32)
        key_frames = frame_of(
            first_row + jnp.arange(keys_block.shape[0], dtype=jnp.int32), frame_ends
        )
        allowed = (key_frames[None, :] <= own_frames[:, None])[None]
        scores = scale * jnp.einsum(
            "qhd,khd->hqk", queries, keys_block, preferred_element_type=jnp.float32
        )
        score_dot = scale * (
            jnp.einsum("qhd,khd->hqk", queries_dot, keys_block, preferred_element_type=jnp.float32)
            + jnp.einsum("qhd,khd->hqk", queries, keys_dot, preferred_element_type=jnp.float32)
        )
        block_max = jnp.max(jnp.where(allowed, scores, neg_large), axis=2)
        new_max = jnp.maximum(run_max, block_max)
        weights = jnp.where(allowed, jnp.exp(scores - new_max[:, :, None]), 0.0)
        rescale = jnp.exp(run_max - new_max)
        weighted_dot = weights * score_dot
        run_total = run_total * rescale + jnp.sum(weights, axis=2)
        run_tan = run_tan * rescale + jnp.sum(weighted_dot, axis=2)
        acc_out = acc_out * rescale[:, :, None] + jnp.einsum(
            "hqk,khd->hqd",
            weights,
            values_wide,
            precision=highest,
            preferred_element_type=jnp.float32,
        )
        acc_tan = (
            acc_tan * rescale[:, :, None]
            + jnp.einsum(
                "hqk,khd->hqd",
                weighted_dot,
                values_wide,
                precision=highest,
                preferred_element_type=jnp.float32,
            )
            + jnp.einsum(
                "hqk,khd->hqd",
                weights,
                values_dot_wide,
                precision=highest,
                preferred_element_type=jnp.float32,
            )
        )
        return (new_max, run_total, run_tan, acc_out, acc_tan)

    row_zeros = jnp.zeros((head_count, local_rows), jnp.float32)
    head_zeros = jnp.zeros((head_count, local_rows, HEAD_DIM), jnp.float32)
    start_state = (
        jnp.full((head_count, local_rows), neg_large, jnp.float32),
        row_zeros,
        row_zeros,
        head_zeros,
        head_zeros,
    )
    run_max, run_total, run_tan, acc_out, acc_tan = over_blocks(
        start_state,
        (
            lax.all_gather(key_proj, "seq", axis=0, tiled=True),
            lax.all_gather(value_proj, "seq", axis=0, tiled=True),
            lax.all_gather(key_tan, "seq", axis=0, tiled=True),
            lax.all_gather(value_tan, "seq", axis=0, tiled=True),
        ),
        forward_step,
    )
    attn = acc_out / run_total[:, :, None]
    mean_tan = run_tan / run_total
    attn_dot = acc_tan / run_total[:, :, None] - mean_tan[:, :, None] * attn
    log_total = run_max + jnp.log(run_total)
    attn16 = flat(jnp.transpose(attn, (1, 0, 2)).astype(jnp.bfloat16))
    attn_dot16 = flat(jnp.transpose(attn_dot, (1, 0, 2)).astype(jnp.bfloat16))
    stacked = jnp.stack([attn16, attn_dot16], axis=1)
    tp_count = lax.axis_size("tp")
    share_rows = local_rows // tp_count
    projected = lax.psum_scatter(
        jnp.einsum("qsf,fd->qsd", stacked, out_weight, preferred_element_type=jnp.float32).astype(
            jnp.bfloat16
        ),
        "tp",
        scatter_dimension=0,
        tiled=True,
    ).astype(jnp.float32)
    branch = projected[:, 0]
    branch_tan = projected[:, 1]
    share_positions = (
        seq_index * local_rows
        + lax.axis_index("tp") * share_rows
        + jnp.arange(share_rows, dtype=jnp.int32)
    )
    share_frames = frame_of(share_positions, frame_ends)
    frame_hits = (
        share_frames[:, None] == jnp.arange(time_index.shape[0], dtype=jnp.int32)[None, :]
    ).astype(jnp.float32)
    levels = jnp.sum(frame_hits * time_index[None, :].astype(jnp.float32), axis=1, keepdims=True)
    angle = (levels + 0.5) * (math.pi / (2 * TSTEPS))
    cosine = jnp.cos(angle)
    sine = jnp.sin(angle)
    target = -(cosine * cosine) * (
        0.5 * branch - latent_velocity.astype(jnp.float32)
    ) - sine * cosine * (noisy_latent.astype(jnp.float32) + 0.5 * branch_tan)
    square_sum = lax.psum(jnp.sum(target * target), ("seq", "tp"))
    mean_square = square_sum / (target.size * lax.axis_size("seq") * lax.axis_size("tp"))
    cotangent = (-target * lax.rsqrt(mean_square + 1e-05)).astype(jnp.bfloat16)
    weight_start = jnp.zeros((local_width, out_weight.shape[1]), jnp.float32)
    piece = lax.all_gather(cotangent, "tp", axis=0, tiled=True)
    weight_grad = weight_start
    row_grad = lax.dot_general(
        piece, out_weight, (((1,), (1,)), ((), ())), preferred_element_type=jnp.float32
    )
    grad_rows = row_grad
    grad_rows, weight_grad = (grad_rows, weight_grad)
    weight_grad = lax.dot_general(
        attn16, piece, (((0,), (0,)), ((), ())), preferred_element_type=jnp.float32
    )
    grad_rows, weight_grad = (grad_rows, weight_grad)
    grad_out_proj = lax.psum_scatter(
        weight_grad.astype(jnp.bfloat16), "seq", scatter_dimension=1, tiled=True
    )
    grad_attn16 = grad_rows.astype(jnp.bfloat16)
    grad_heads = heads(grad_attn16)
    dterm = jnp.transpose(
        jnp.sum(grad_heads.astype(jnp.float32) * heads(attn16).astype(jnp.float32), axis=2)
    )

    def backward_block(
        query_heads,
        grad_block,
        query_lse,
        query_dterm,
        query_frames,
        key_heads,
        value_heads,
        key_frames,
    ):
        allowed = (key_frames[None, :] <= query_frames[:, None])[None]
        scores = scale * jnp.einsum(
            "qhd,khd->hqk", query_heads, key_heads, preferred_element_type=jnp.float32
        )
        probs = jnp.where(allowed, jnp.exp(scores - query_lse[:, :, None]), 0.0)
        probs16 = probs.astype(jnp.bfloat16)
        value_grad = jnp.einsum(
            "hqk,qhd->khd", probs16, grad_block, preferred_element_type=jnp.float32
        )
        prob_grad = jnp.einsum(
            "qhd,khd->hqk", grad_block, value_heads, preferred_element_type=jnp.float32
        )
        score_grad = (probs * (prob_grad - query_dterm[:, :, None])).astype(jnp.bfloat16)
        query_grad = scale * jnp.einsum(
            "hqk,khd->qhd", score_grad, key_heads, preferred_element_type=jnp.float32
        )
        key_grad = scale * jnp.einsum(
            "hqk,qhd->khd", score_grad, query_heads, preferred_element_type=jnp.float32
        )
        return (query_grad, key_grad, value_grad)

    grad_zeros = jnp.zeros((local_rows, head_count, HEAD_DIM), jnp.float32)

    def cycle_step(step, state):
        moving_keys, moving_values, key_acc, value_acc, query_acc = state
        source = (seq_index - step) % cycle_length
        source_frames = frame_of(source * local_rows + row_offsets, frame_ends)
        query_grad, key_grad, value_grad = backward_block(
            queries,
            grad_heads,
            log_total,
            dterm,
            own_frames,
            heads(moving_keys),
            heads(moving_values),
            source_frames,
        )
        key_acc = key_acc + key_grad
        value_acc = value_acc + value_grad
        query_acc = query_acc + query_grad
        moving_keys, moving_values = shifted((moving_keys, moving_values), "seq", 1)
        key_acc, value_acc = (
            shifted(key_acc.astype(jnp.bfloat16), "seq", 1).astype(key_acc.dtype),
            shifted(value_acc.astype(jnp.bfloat16), "seq", 1).astype(value_acc.dtype),
        )
        return (moving_keys, moving_values, key_acc, value_acc, query_acc)

    final_state = lax.fori_loop(
        0, cycle_length, cycle_step, (key_proj, value_proj, grad_zeros, grad_zeros, grad_zeros)
    )
    key_total, value_total, query_total = (final_state[2], final_state[3], final_state[4])
    return (
        flat(query_total).astype(jnp.bfloat16),
        flat(key_total).astype(jnp.bfloat16),
        flat(value_total).astype(jnp.bfloat16),
        grad_out_proj,
    )


def solution(mesh):
    in_specs = (
        P("seq", "tp"),
        P("seq", "tp"),
        P("seq", "tp"),
        P("seq", "tp"),
        P("seq", "tp"),
        P("seq", "tp"),
        P("tp", None),
        P(("seq", "tp"), None),
        P(("seq", "tp"), None),
        P(),
        P(),
    )
    out_specs = (P("seq", "tp"), P("seq", "tp"), P("seq", "tp"), P("tp", "seq"))
    return jax.shard_map(
        on_device, mesh=mesh, in_specs=in_specs, out_specs=out_specs, check_vma=False
    )
```

profile of v0, /device:TPU:1, one launch (start us, length us, event | category | flops | bytes accessed | tf_op | source)
XLA Modules:
  0.0 706.2 jit_solution(648920528121839479)
XLA Ops:
  16.2 32.9 %all-gather.11.cloned.1.call-done = bf16[2560,512]{1,0:T(8,128)(2,1)} async-done(((bf16[160,512]{1,0:T(8,128)(2,1)}), bf16[2560,512]{1,0:T(8,128)(2,1)}) %all-gather.11.cloned.1.call-update) | async-done | bytes 2621456 | tf_op jit(solution)/shard_map/all_gather | solution.py:140
  49.1 37.2 %all-gather.7.cloned.1.call-done = bf16[2560,512]{1,0:T(8,128)(2,1)} async-done(((bf16[160,512]{1,0:T(8,128)(2,1)}), bf16[2560,512]{1,0:T(8,128)(2,1)}) %all-gather.7.cloned.1.call-update) | async-done | bytes 2621456 | tf_op jit(solution)/shard_map/all_gather | solution.py:139
  86.3 36.6 %all-gather.13.cloned.1.call-done = bf16[2560,512]{1,0:T(8,128)(2,1)} async-done(((bf16[160,512]{1,0:T(8,128)(2,1)}), bf16[2560,512]{1,0:T(8,128)(2,1)}) %all-gather.13.cloned.1.call-update) | async-done | bytes 2621456 | tf_op jit(solution)/shard_map/all_gather | solution.py:142
  122.9 36.5 %all-gather.9.cloned.1.call-done = bf16[2560,512]{1,0:T(8,128)(2,1)} async-done(((bf16[160,512]{1,0:T(8,128)(2,1)}), bf16[2560,512]{1,0:T(8,128)(2,1)}) %all-gather.9.cloned.1.call-update) | async-done | bytes 2621456 | tf_op jit(solution)/shard_map/all_gather | solution.py:141
  159.4 97.0 %while.46 = (s32[]{:T(128)}, f32[4,160]{1,0:T(4,128)S(1)}, f32[4,160]{1,0:T(4,128)}, f32[4,160]{1,0:T(4,128)}, f32[4,160,128]{2,1,0:T(8,128)}, /*index=5*/f32[4,...) while((s32[]{:T(128)}, f32[4,160]{1,0:T(4,128)S(1)}, ...), condition=%wide.region_7.8_spmd.clone, body=%wide.region_2.7_spmd.clone.sunk | while | flops 2210912768 | bytes 40213724 | solution.py:43
  173.5 2.7 convolution_add_fusion.7
  177.7 3.1 convolution_add_fusion.8
  197.7 2.8 convolution_add_fusion.7
  201.9 3.1 convolution_add_fusion.8
  222.0 2.8 convolution_add_fusion.7
  226.2 3.1 convolution_add_fusion.8
  246.3 2.8 convolution_add_fusion.7
  250.5 3.1 convolution_add_fusion.8
  258.7 3.7 convolution_convert_fusion.1
  262.4 4.3 copy.105
  269.4 89.3 %all-reduce.3.cloned.1.call-done = bf16[160,2,4096]{2,1,0:T(2,128)(2,1)} async-done(((bf16[160,2,4096]{2,1,0:T(2,128)(2,1)}), bf16[160,2,4096]{2,1,0:T(2,128)(2,1)}) %all-reduce.3.cloned.1.call-update) | async-done | bytes 2621456
  361.8 67.5 %psum.7 = f32[]{:T(128)} all-reduce(f32[]{:T(128)} %get-tuple-element.817), channel_id=1, replica_groups=mesh['seq'=16,'tp'=8] {'seq','tp'}, use_global_device_ids=true, to_apply=%region_12.13 | all-reduce | flops 1 | bytes 8 | tf_op jit(solution)/shard_map/psum | solution.py:181
  430.8 46.6 %all-gather.15.cloned.1.call-done = bf16[8,20,4096]{2,1,0:T(8,128)(2,1)} async-done(((bf16[1,20,4096]{2,1,0:T(8,128)(2,1)}), bf16[8,20,4096]{2,1,0:T(8,128)(2,1)}) %all-gather.15.cloned.1.call-update) | async-done | bytes 1310736 | tf_op jit(solution)/shard_map/all_gather | solution.py:185
  479.8 4.6 convolution_convert_fusion
  484.3 4.1 fusion.34
  489.7 207.6 %while.47 = (s32[]{:T(128)}, bf16[160,512]{1,0:T(8,128)(2,1)S(1)}, bf16[160,512]{1,0:T(8,128)(2,1)S(1)}, f32[160,4,128]{2,0,1:T(8,128)S(1)}, f32[160,4,128]{2,0,...) while((s32[]{:T(128)}, bf16[160,512]{1,0:T(8,128)(2,1)S(1)}, ...), condition=%wide.region_16.17_spmd.clone, body=%wide.region_14.16_spmd.clone.sunk | while | flops 132805136 | bytes 8948378 | solution.py:262
  496.7 4.3 collective-permute-done.2
  501.1 2.8 collective-permute-done.3
  504.0 2.5 collective-permute-start
  510.3 7.1 %collective-permute-done.2 = bf16[160,4,128]{2,0,1:T(8,128)(2,1)S(1)} collective-permute-done((bf16[160,4,128]{2,0,1:T(8,128)(2,1)S(1)}, bf16[160,4,128]{2,0,1:T(8,128)(2,1)S(1)}, u32[]{:S(2)}, u32[]{:S(2)}) %collective-permute-start.2) | collective-permute-done | bytes 163872 | tf_op jit(solution)/shard_map/while/body/eval_jaxpr/ppermute | solution.py:17
  519.3 2.5 collective-permute-start
  525.1 6.1 collective-permute-done.2
  533.0 2.5 collective-permute-start
  538.8 6.7 collective-permute-done.2
  547.3 2.5 collective-permute-start
  553.1 7.8 %collective-permute-done.2 = bf16[160,4,128]{2,0,1:T(8,128)(2,1)S(1)} collective-permute-done((bf16[160,4,128]{2,0,1:T(8,128)(2,1)S(1)}, bf16[160,4,128]{2,0,1:T(8,128)(2,1)S(1)}, u32[]{:S(2)}, u32[]{:S(2)}) %collective-permute-start.2) | collective-permute-done | bytes 163872 | tf_op jit(solution)/shard_map/while/body/eval_jaxpr/ppermute | solution.py:17
  562.7 2.5 collective-permute-start
  569.2 6.9 collective-permute-done.2
  578.3 2.5 collective-permute-start
  585.2 5.7 collective-permute-done.2
  592.7 2.5 collective-permute-start
  598.5 3.9 collective-permute-done.2
  604.3 2.5 collective-permute-start
  624.6 2.5 collective-permute-start
  631.9 3.5 collective-permute-done.2
  643.0 4.7 collective-permute-done.2
  654.1 5.9 collective-permute-done.2
  663.0 2.8 collective-permute-start.2
  666.5 5.7 collective-permute-done.2
  675.3 2.9 collective-permute-start.2
  678.9 5.6 collective-permute-done.2
  687.6 2.8 collective-permute-start.2
  691.2 5.7 collective-permute-done.2
  (520 shorter events, 187.1 us)
Async XLA Ops:
  7.2 41.9 %all-gather.11.cloned.1.call-start = ((), (), s32[]{:S(2)}) async-start(), calls=%async_computation.3 | async-start | bytes 2785280 | tf_op jit(solution)/shard_map/all_gather | solution.py:140
  10.5 75.8 %all-gather.7.cloned.1.call-start = ((), (), s32[]{:S(2)}) async-start(), calls=%async_computation.1 | async-start | bytes 2785280 | tf_op jit(solution)/shard_map/all_gather | solution.py:139
  11.2 111.7 %all-gather.13.cloned.1.call-start = ((), (), s32[]{:S(2)}) async-start(), calls=%async_computation.4 | async-start | bytes 2785280 | tf_op jit(solution)/shard_map/all_gather | solution.py:142
  12.0 147.4 %all-gather.9.cloned.1.call-start = ((), (), s32[]{:S(2)}) async-start(), calls=%async_computation.2 | async-start | bytes 2785280 | tf_op jit(solution)/shard_map/all_gather | solution.py:141
  12.5 346.2 %all-reduce.3.cloned.1.call-start = ((), (), s32[]{:S(2)}) async-start(), calls=%async_computation.7 | async-start | bytes 5242880
  266.7 210.7 %all-gather.15.cloned.1.call-start = ((), (), s32[]{:S(2)}) async-start(), calls=%async_computation.6 | async-start | bytes 1769472 | tf_op jit(solution)/shard_map/all_gather | solution.py:185
  430.7 268.6 %reduce-scatter.2.cloned.1.call-start = ((), (), s32[]{:S(2)}) async-start(), calls=%async_computation.5 | async-start | bytes 4456448 | tf_op jit(solution)/shard_map/reduce_scatter | solution.py:196
  489.8 14.2 %collective-permute-start = (bf16[160,512]{1,0:T(8,128)(2,1)S(1)}, bf16[160,512]{1,0:T(8,128)(2,1)S(1)}, u32[]{:S(2)}, u32[]{:S(2)}) collective-permute-start(bf16[160,512]{1,0:T(8,128)(2,1)S(1)} %copy.215), channel_id=1, source_target_pairs={{0,8},{8,16},{16,24},{24,32},{32,40},{40,48},{48,56},{56,64},{64,7... | collective-permute-start | bytes 491528 | tf_op jit(solution)/shard_map/while/body/eval_jaxpr/ppermute | solution.py:17
  491.1 12.8 %collective-permute-start.1 = (bf16[160,512]{1,0:T(8,128)(2,1)S(1)}, bf16[160,512]{1,0:T(8,128)(2,1)S(1)}, u32[]{:S(2)}, u32[]{:S(2)}) collective-permute-start(bf16[160,512]{1,0:T(8,128)(2,1)S(1)} %copy.216), channel_id=1, source_target_pairs={{0,8},{8,16},{16,24},{24,32},{32,40},{40,48},{48,56},{56,64},{64,7... | collective-permute-start | bytes 491528 | tf_op jit(solution)/shard_map/while/body/eval_jaxpr/ppermute | solution.py:17
  504.0 15.3 %collective-permute-start = (bf16[160,512]{1,0:T(8,128)(2,1)S(1)}, bf16[160,512]{1,0:T(8,128)(2,1)S(1)}, u32[]{:S(2)}, u32[]{:S(2)}) collective-permute-start(bf16[160,512]{1,0:T(8,128)(2,1)S(1)} %copy.215), channel_id=1, source_target_pairs={{0,8},{8,16},{16,24},{24,32},{32,40},{40,48},{48,56},{56,64},{64,7... | collective-permute-start | bytes 491528 | tf_op jit(solution)/shard_map/while/body/eval_jaxpr/ppermute | solution.py:17
  506.5 12.7 %collective-permute-start.1 = (bf16[160,512]{1,0:T(8,128)(2,1)S(1)}, bf16[160,512]{1,0:T(8,128)(2,1)S(1)}, u32[]{:S(2)}, u32[]{:S(2)}) collective-permute-start(bf16[160,512]{1,0:T(8,128)(2,1)S(1)} %copy.216), channel_id=1, source_target_pairs={{0,8},{8,16},{16,24},{24,32},{32,40},{40,48},{48,56},{56,64},{64,7... | collective-permute-start | bytes 491528 | tf_op jit(solution)/shard_map/while/body/eval_jaxpr/ppermute | solution.py:17
  508.9 8.6 %collective-permute-start.2 = (bf16[160,4,128]{2,0,1:T(8,128)(2,1)S(1)}, bf16[160,4,128]{2,0,1:T(8,128)(2,1)S(1)}, u32[]{:S(2)}, u32[]{:S(2)}) collective-permute-start(bf16[160,4,128]{2,0,1:T(8,128)(2,1)S(1)} %fusion.149), channel_id=1, source_target_pairs={{0,8},{8,16},{16,24},{24,32},{32,40},{40,48},{48,56},{56,64},{64,7... | collective-permute-start | bytes 491528 | tf_op jit(solution)/shard_map/while/body/eval_jaxpr/ppermute | solution.py:17
  509.8 9.5 %collective-permute-start.3 = (bf16[160,4,128]{2,0,1:T(8,128)(2,1)S(1)}, bf16[160,4,128]{2,0,1:T(8,128)(2,1)S(1)}, u32[]{:S(2)}, u32[]{:S(2)}) collective-permute-start(bf16[160,4,128]{2,0,1:T(8,128)(2,1)S(1)} %fusion.150), channel_id=1, source_target_pairs={{0,8},{8,16},{16,24},{24,32},{32,40},{40,48},{48,56},{56,64},{64,7... | collective-permute-start | bytes 491528 | tf_op jit(solution)/shard_map/while/body/eval_jaxpr/ppermute | solution.py:17
  519.3 13.6 %collective-permute-start = (bf16[160,512]{1,0:T(8,128)(2,1)S(1)}, bf16[160,512]{1,0:T(8,128)(2,1)S(1)}, u32[]{:S(2)}, u32[]{:S(2)}) collective-permute-start(bf16[160,512]{1,0:T(8,128)(2,1)S(1)} %copy.215), channel_id=1, source_target_pairs={{0,8},{8,16},{16,24},{24,32},{32,40},{40,48},{48,56},{56,64},{64,7... | collective-permute-start | bytes 491528 | tf_op jit(solution)/shard_map/while/body/eval_jaxpr/ppermute | solution.py:17
  521.9 11.1 %collective-permute-start.1 = (bf16[160,512]{1,0:T(8,128)(2,1)S(1)}, bf16[160,512]{1,0:T(8,128)(2,1)S(1)}, u32[]{:S(2)}, u32[]{:S(2)}) collective-permute-start(bf16[160,512]{1,0:T(8,128)(2,1)S(1)} %copy.216), channel_id=1, source_target_pairs={{0,8},{8,16},{16,24},{24,32},{32,40},{40,48},{48,56},{56,64},{64,7... | collective-permute-start | bytes 491528 | tf_op jit(solution)/shard_map/while/body/eval_jaxpr/ppermute | solution.py:17
  533.0 14.3 %collective-permute-start = (bf16[160,512]{1,0:T(8,128)(2,1)S(1)}, bf16[160,512]{1,0:T(8,128)(2,1)S(1)}, u32[]{:S(2)}, u32[]{:S(2)}) collective-permute-start(bf16[160,512]{1,0:T(8,128)(2,1)S(1)} %copy.215), channel_id=1, source_target_pairs={{0,8},{8,16},{16,24},{24,32},{32,40},{40,48},{48,56},{56,64},{64,7... | collective-permute-start | bytes 491528 | tf_op jit(solution)/shard_map/while/body/eval_jaxpr/ppermute | solution.py:17
  535.6 11.7 %collective-permute-start.1 = (bf16[160,512]{1,0:T(8,128)(2,1)S(1)}, bf16[160,512]{1,0:T(8,128)(2,1)S(1)}, u32[]{:S(2)}, u32[]{:S(2)}) collective-permute-start(bf16[160,512]{1,0:T(8,128)(2,1)S(1)} %copy.216), channel_id=1, source_target_pairs={{0,8},{8,16},{16,24},{24,32},{32,40},{40,48},{48,56},{56,64},{64,7... | collective-permute-start | bytes 491528 | tf_op jit(solution)/shard_map/while/body/eval_jaxpr/ppermute | solution.py:17
  538.4 8.9 %collective-permute-start.3 = (bf16[160,4,128]{2,0,1:T(8,128)(2,1)S(1)}, bf16[160,4,128]{2,0,1:T(8,128)(2,1)S(1)}, u32[]{:S(2)}, u32[]{:S(2)}) collective-permute-start(bf16[160,4,128]{2,0,1:T(8,128)(2,1)S(1)} %fusion.150), channel_id=1, source_target_pairs={{0,8},{8,16},{16,24},{24,32},{32,40},{40,48},{48,56},{56,64},{64,7... | collective-permute-start | bytes 491528 | tf_op jit(solution)/shard_map/while/body/eval_jaxpr/ppermute | solution.py:17
  547.3 15.4 %collective-permute-start = (bf16[160,512]{1,0:T(8,128)(2,1)S(1)}, bf16[160,512]{1,0:T(8,128)(2,1)S(1)}, u32[]{:S(2)}, u32[]{:S(2)}) collective-permute-start(bf16[160,512]{1,0:T(8,128)(2,1)S(1)} %copy.215), channel_id=1, source_target_pairs={{0,8},{8,16},{16,24},{24,32},{32,40},{40,48},{48,56},{56,64},{64,7... | collective-permute-start | bytes 491528 | tf_op jit(solution)/shard_map/while/body/eval_jaxpr/ppermute | solution.py:17
  549.9 12.8 %collective-permute-start.1 = (bf16[160,512]{1,0:T(8,128)(2,1)S(1)}, bf16[160,512]{1,0:T(8,128)(2,1)S(1)}, u32[]{:S(2)}, u32[]{:S(2)}) collective-permute-start(bf16[160,512]{1,0:T(8,128)(2,1)S(1)} %copy.216), channel_id=1, source_target_pairs={{0,8},{8,16},{16,24},{24,32},{32,40},{40,48},{48,56},{56,64},{64,7... | collective-permute-start | bytes 491528 | tf_op jit(solution)/shard_map/while/body/eval_jaxpr/ppermute | solution.py:17
  552.3 8.6 %collective-permute-start.2 = (bf16[160,4,128]{2,0,1:T(8,128)(2,1)S(1)}, bf16[160,4,128]{2,0,1:T(8,128)(2,1)S(1)}, u32[]{:S(2)}, u32[]{:S(2)}) collective-permute-start(bf16[160,4,128]{2,0,1:T(8,128)(2,1)S(1)} %fusion.149), channel_id=1, source_target_pairs={{0,8},{8,16},{16,24},{24,32},{32,40},{40,48},{48,56},{56,64},{64,7... | collective-permute-start | bytes 491528 | tf_op jit(solution)/shard_map/while/body/eval_jaxpr/ppermute | solution.py:17
  552.7 9.9 %collective-permute-start.3 = (bf16[160,4,128]{2,0,1:T(8,128)(2,1)S(1)}, bf16[160,4,128]{2,0,1:T(8,128)(2,1)S(1)}, u32[]{:S(2)}, u32[]{:S(2)}) collective-permute-start(bf16[160,4,128]{2,0,1:T(8,128)(2,1)S(1)} %fusion.150), channel_id=1, source_target_pairs={{0,8},{8,16},{16,24},{24,32},{32,40},{40,48},{48,56},{56,64},{64,7... | collective-permute-start | bytes 491528 | tf_op jit(solution)/shard_map/while/body/eval_jaxpr/ppermute | solution.py:17
  562.7 15.5 %collective-permute-start = (bf16[160,512]{1,0:T(8,128)(2,1)S(1)}, bf16[160,512]{1,0:T(8,128)(2,1)S(1)}, u32[]{:S(2)}, u32[]{:S(2)}) collective-permute-start(bf16[160,512]{1,0:T(8,128)(2,1)S(1)} %copy.215), channel_id=1, source_target_pairs={{0,8},{8,16},{16,24},{24,32},{32,40},{40,48},{48,56},{56,64},{64,7... | collective-permute-start | bytes 491528 | tf_op jit(solution)/shard_map/while/body/eval_jaxpr/ppermute | solution.py:17
  565.3 12.9 %collective-permute-start.1 = (bf16[160,512]{1,0:T(8,128)(2,1)S(1)}, bf16[160,512]{1,0:T(8,128)(2,1)S(1)}, u32[]{:S(2)}, u32[]{:S(2)}) collective-permute-start(bf16[160,512]{1,0:T(8,128)(2,1)S(1)} %copy.216), channel_id=1, source_target_pairs={{0,8},{8,16},{16,24},{24,32},{32,40},{40,48},{48,56},{56,64},{64,7... | collective-permute-start | bytes 491528 | tf_op jit(solution)/shard_map/while/body/eval_jaxpr/ppermute | solution.py:17
  568.1 10.0 %collective-permute-start.3 = (bf16[160,4,128]{2,0,1:T(8,128)(2,1)S(1)}, bf16[160,4,128]{2,0,1:T(8,128)(2,1)S(1)}, u32[]{:S(2)}, u32[]{:S(2)}) collective-permute-start(bf16[160,4,128]{2,0,1:T(8,128)(2,1)S(1)} %fusion.150), channel_id=1, source_target_pairs={{0,8},{8,16},{16,24},{24,32},{32,40},{40,48},{48,56},{56,64},{64,7... | collective-permute-start | bytes 491528 | tf_op jit(solution)/shard_map/while/body/eval_jaxpr/ppermute | solution.py:17
  578.3 14.4 %collective-permute-start = (bf16[160,512]{1,0:T(8,128)(2,1)S(1)}, bf16[160,512]{1,0:T(8,128)(2,1)S(1)}, u32[]{:S(2)}, u32[]{:S(2)}) collective-permute-start(bf16[160,512]{1,0:T(8,128)(2,1)S(1)} %copy.215), channel_id=1, source_target_pairs={{0,8},{8,16},{16,24},{24,32},{32,40},{40,48},{48,56},{56,64},{64,7... | collective-permute-start | bytes 491528 | tf_op jit(solution)/shard_map/while/body/eval_jaxpr/ppermute | solution.py:17
  580.8 11.9 %collective-permute-start.1 = (bf16[160,512]{1,0:T(8,128)(2,1)S(1)}, bf16[160,512]{1,0:T(8,128)(2,1)S(1)}, u32[]{:S(2)}, u32[]{:S(2)}) collective-permute-start(bf16[160,512]{1,0:T(8,128)(2,1)S(1)} %copy.216), channel_id=1, source_target_pairs={{0,8},{8,16},{16,24},{24,32},{32,40},{40,48},{48,56},{56,64},{64,7... | collective-permute-start | bytes 491528 | tf_op jit(solution)/shard_map/while/body/eval_jaxpr/ppermute | solution.py:17
  583.6 9.0 %collective-permute-start.3 = (bf16[160,4,128]{2,0,1:T(8,128)(2,1)S(1)}, bf16[160,4,128]{2,0,1:T(8,128)(2,1)S(1)}, u32[]{:S(2)}, u32[]{:S(2)}) collective-permute-start(bf16[160,4,128]{2,0,1:T(8,128)(2,1)S(1)} %fusion.150), channel_id=1, source_target_pairs={{0,8},{8,16},{16,24},{24,32},{32,40},{40,48},{48,56},{56,64},{64,7... | collective-permute-start | bytes 491528 | tf_op jit(solution)/shard_map/while/body/eval_jaxpr/ppermute | solution.py:17
  592.7 11.5 %collective-permute-start = (bf16[160,512]{1,0:T(8,128)(2,1)S(1)}, bf16[160,512]{1,0:T(8,128)(2,1)S(1)}, u32[]{:S(2)}, u32[]{:S(2)}) collective-permute-start(bf16[160,512]{1,0:T(8,128)(2,1)S(1)} %copy.215), channel_id=1, source_target_pairs={{0,8},{8,16},{16,24},{24,32},{32,40},{40,48},{48,56},{56,64},{64,7... | collective-permute-start | bytes 491528 | tf_op jit(solution)/shard_map/while/body/eval_jaxpr/ppermute | solution.py:17
  595.3 9.0 %collective-permute-start.1 = (bf16[160,512]{1,0:T(8,128)(2,1)S(1)}, bf16[160,512]{1,0:T(8,128)(2,1)S(1)}, u32[]{:S(2)}, u32[]{:S(2)}) collective-permute-start(bf16[160,512]{1,0:T(8,128)(2,1)S(1)} %copy.216), channel_id=1, source_target_pairs={{0,8},{8,16},{16,24},{24,32},{32,40},{40,48},{48,56},{56,64},{64,7... | collective-permute-start | bytes 491528 | tf_op jit(solution)/shard_map/while/body/eval_jaxpr/ppermute | solution.py:17
  604.3 10.1 %collective-permute-start = (bf16[160,512]{1,0:T(8,128)(2,1)S(1)}, bf16[160,512]{1,0:T(8,128)(2,1)S(1)}, u32[]{:S(2)}, u32[]{:S(2)}) collective-permute-start(bf16[160,512]{1,0:T(8,128)(2,1)S(1)} %copy.215), channel_id=1, source_target_pairs={{0,8},{8,16},{16,24},{24,32},{32,40},{40,48},{48,56},{56,64},{64,7... | collective-permute-start | bytes 491528 | tf_op jit(solution)/shard_map/while/body/eval_jaxpr/ppermute | solution.py:17
  614.5 10.1 %collective-permute-start = (bf16[160,512]{1,0:T(8,128)(2,1)S(1)}, bf16[160,512]{1,0:T(8,128)(2,1)S(1)}, u32[]{:S(2)}, u32[]{:S(2)}) collective-permute-start(bf16[160,512]{1,0:T(8,128)(2,1)S(1)} %copy.215), channel_id=1, source_target_pairs={{0,8},{8,16},{16,24},{24,32},{32,40},{40,48},{48,56},{56,64},{64,7... | collective-permute-start | bytes 491528 | tf_op jit(solution)/shard_map/while/body/eval_jaxpr/ppermute | solution.py:17
  624.6 11.3 %collective-permute-start = (bf16[160,512]{1,0:T(8,128)(2,1)S(1)}, bf16[160,512]{1,0:T(8,128)(2,1)S(1)}, u32[]{:S(2)}, u32[]{:S(2)}) collective-permute-start(bf16[160,512]{1,0:T(8,128)(2,1)S(1)} %copy.215), channel_id=1, source_target_pairs={{0,8},{8,16},{16,24},{24,32},{32,40},{40,48},{48,56},{56,64},{64,7... | collective-permute-start | bytes 491528 | tf_op jit(solution)/shard_map/while/body/eval_jaxpr/ppermute | solution.py:17
  627.2 8.7 %collective-permute-start.1 = (bf16[160,512]{1,0:T(8,128)(2,1)S(1)}, bf16[160,512]{1,0:T(8,128)(2,1)S(1)}, u32[]{:S(2)}, u32[]{:S(2)}) collective-permute-start(bf16[160,512]{1,0:T(8,128)(2,1)S(1)} %copy.216), channel_id=1, source_target_pairs={{0,8},{8,16},{16,24},{24,32},{32,40},{40,48},{48,56},{56,64},{64,7... | collective-permute-start | bytes 491528 | tf_op jit(solution)/shard_map/while/body/eval_jaxpr/ppermute | solution.py:17
  636.0 12.2 %collective-permute-start = (bf16[160,512]{1,0:T(8,128)(2,1)S(1)}, bf16[160,512]{1,0:T(8,128)(2,1)S(1)}, u32[]{:S(2)}, u32[]{:S(2)}) collective-permute-start(bf16[160,512]{1,0:T(8,128)(2,1)S(1)} %copy.215), channel_id=1, source_target_pairs={{0,8},{8,16},{16,24},{24,32},{32,40},{40,48},{48,56},{56,64},{64,7... | collective-permute-start | bytes 491528 | tf_op jit(solution)/shard_map/while/body/eval_jaxpr/ppermute | solution.py:17
  637.8 10.4 %collective-permute-start.1 = (bf16[160,512]{1,0:T(8,128)(2,1)S(1)}, bf16[160,512]{1,0:T(8,128)(2,1)S(1)}, u32[]{:S(2)}, u32[]{:S(2)}) collective-permute-start(bf16[160,512]{1,0:T(8,128)(2,1)S(1)} %copy.216), channel_id=1, source_target_pairs={{0,8},{8,16},{16,24},{24,32},{32,40},{40,48},{48,56},{56,64},{64,7... | collective-permute-start | bytes 491528 | tf_op jit(solution)/shard_map/while/body/eval_jaxpr/ppermute | solution.py:17
  648.2 12.2 %collective-permute-start = (bf16[160,512]{1,0:T(8,128)(2,1)S(1)}, bf16[160,512]{1,0:T(8,128)(2,1)S(1)}, u32[]{:S(2)}, u32[]{:S(2)}) collective-permute-start(bf16[160,512]{1,0:T(8,128)(2,1)S(1)} %copy.215), channel_id=1, source_target_pairs={{0,8},{8,16},{16,24},{24,32},{32,40},{40,48},{48,56},{56,64},{64,7... | collective-permute-start | bytes 491528 | tf_op jit(solution)/shard_map/while/body/eval_jaxpr/ppermute | solution.py:17
  648.9 11.6 %collective-permute-start.1 = (bf16[160,512]{1,0:T(8,128)(2,1)S(1)}, bf16[160,512]{1,0:T(8,128)(2,1)S(1)}, u32[]{:S(2)}, u32[]{:S(2)}) collective-permute-start(bf16[160,512]{1,0:T(8,128)(2,1)S(1)} %copy.216), channel_id=1, source_target_pairs={{0,8},{8,16},{16,24},{24,32},{32,40},{40,48},{48,56},{56,64},{64,7... | collective-permute-start | bytes 491528 | tf_op jit(solution)/shard_map/while/body/eval_jaxpr/ppermute | solution.py:17
  651.3 8.7 %collective-permute-start.2 = (bf16[160,4,128]{2,0,1:T(8,128)(2,1)S(1)}, bf16[160,4,128]{2,0,1:T(8,128)(2,1)S(1)}, u32[]{:S(2)}, u32[]{:S(2)}) collective-permute-start(bf16[160,4,128]{2,0,1:T(8,128)(2,1)S(1)} %fusion.149), channel_id=1, source_target_pairs={{0,8},{8,16},{16,24},{24,32},{32,40},{40,48},{48,56},{56,64},{64,7... | collective-permute-start | bytes 491528 | tf_op jit(solution)/shard_map/while/body/eval_jaxpr/ppermute | solution.py:17
  660.5 12.2 %collective-permute-start = (bf16[160,512]{1,0:T(8,128)(2,1)S(1)}, bf16[160,512]{1,0:T(8,128)(2,1)S(1)}, u32[]{:S(2)}, u32[]{:S(2)}) collective-permute-start(bf16[160,512]{1,0:T(8,128)(2,1)S(1)} %copy.215), channel_id=1, source_target_pairs={{0,8},{8,16},{16,24},{24,32},{32,40},{40,48},{48,56},{56,64},{64,7... | collective-permute-start | bytes 491528 | tf_op jit(solution)/shard_map/while/body/eval_jaxpr/ppermute | solution.py:17
  660.6 12.1 %collective-permute-start.1 = (bf16[160,512]{1,0:T(8,128)(2,1)S(1)}, bf16[160,512]{1,0:T(8,128)(2,1)S(1)}, u32[]{:S(2)}, u32[]{:S(2)}) collective-permute-start(bf16[160,512]{1,0:T(8,128)(2,1)S(1)} %copy.216), channel_id=1, source_target_pairs={{0,8},{8,16},{16,24},{24,32},{32,40},{40,48},{48,56},{56,64},{64,7... | collective-permute-start | bytes 491528 | tf_op jit(solution)/shard_map/while/body/eval_jaxpr/ppermute | solution.py:17
  663.0 9.3 %collective-permute-start.2 = (bf16[160,4,128]{2,0,1:T(8,128)(2,1)S(1)}, bf16[160,4,128]{2,0,1:T(8,128)(2,1)S(1)}, u32[]{:S(2)}, u32[]{:S(2)}) collective-permute-start(bf16[160,4,128]{2,0,1:T(8,128)(2,1)S(1)} %fusion.149), channel_id=1, source_target_pairs={{0,8},{8,16},{16,24},{24,32},{32,40},{40,48},{48,56},{56,64},{64,7... | collective-permute-start | bytes 491528 | tf_op jit(solution)/shard_map/while/body/eval_jaxpr/ppermute | solution.py:17
  672.8 12.2 %collective-permute-start = (bf16[160,512]{1,0:T(8,128)(2,1)S(1)}, bf16[160,512]{1,0:T(8,128)(2,1)S(1)}, u32[]{:S(2)}, u32[]{:S(2)}) collective-permute-start(bf16[160,512]{1,0:T(8,128)(2,1)S(1)} %copy.215), channel_id=1, source_target_pairs={{0,8},{8,16},{16,24},{24,32},{32,40},{40,48},{48,56},{56,64},{64,7... | collective-permute-start | bytes 491528 | tf_op jit(solution)/shard_map/while/body/eval_jaxpr/ppermute | solution.py:17
  672.9 12.1 %collective-permute-start.1 = (bf16[160,512]{1,0:T(8,128)(2,1)S(1)}, bf16[160,512]{1,0:T(8,128)(2,1)S(1)}, u32[]{:S(2)}, u32[]{:S(2)}) collective-permute-start(bf16[160,512]{1,0:T(8,128)(2,1)S(1)} %copy.216), channel_id=1, source_target_pairs={{0,8},{8,16},{16,24},{24,32},{32,40},{40,48},{48,56},{56,64},{64,7... | collective-permute-start | bytes 491528 | tf_op jit(solution)/shard_map/while/body/eval_jaxpr/ppermute | solution.py:17
  675.3 9.3 %collective-permute-start.2 = (bf16[160,4,128]{2,0,1:T(8,128)(2,1)S(1)}, bf16[160,4,128]{2,0,1:T(8,128)(2,1)S(1)}, u32[]{:S(2)}, u32[]{:S(2)}) collective-permute-start(bf16[160,4,128]{2,0,1:T(8,128)(2,1)S(1)} %fusion.149), channel_id=1, source_target_pairs={{0,8},{8,16},{16,24},{24,32},{32,40},{40,48},{48,56},{56,64},{64,7... | collective-permute-start | bytes 491528 | tf_op jit(solution)/shard_map/while/body/eval_jaxpr/ppermute | solution.py:17
  685.0 12.2 %collective-permute-start = (bf16[160,512]{1,0:T(8,128)(2,1)S(1)}, bf16[160,512]{1,0:T(8,128)(2,1)S(1)}, u32[]{:S(2)}, u32[]{:S(2)}) collective-permute-start(bf16[160,512]{1,0:T(8,128)(2,1)S(1)} %copy.215), channel_id=1, source_target_pairs={{0,8},{8,16},{16,24},{24,32},{32,40},{40,48},{48,56},{56,64},{64,7... | collective-permute-start | bytes 491528 | tf_op jit(solution)/shard_map/while/body/eval_jaxpr/ppermute | solution.py:17
  685.2 12.1 %collective-permute-start.1 = (bf16[160,512]{1,0:T(8,128)(2,1)S(1)}, bf16[160,512]{1,0:T(8,128)(2,1)S(1)}, u32[]{:S(2)}, u32[]{:S(2)}) collective-permute-start(bf16[160,512]{1,0:T(8,128)(2,1)S(1)} %copy.216), channel_id=1, source_target_pairs={{0,8},{8,16},{16,24},{24,32},{32,40},{40,48},{48,56},{56,64},{64,7... | collective-permute-start | bytes 491528 | tf_op jit(solution)/shard_map/while/body/eval_jaxpr/ppermute | solution.py:17
  687.6 9.3 %collective-permute-start.2 = (bf16[160,4,128]{2,0,1:T(8,128)(2,1)S(1)}, bf16[160,4,128]{2,0,1:T(8,128)(2,1)S(1)}, u32[]{:S(2)}, u32[]{:S(2)}) collective-permute-start(bf16[160,4,128]{2,0,1:T(8,128)(2,1)S(1)} %fusion.149), channel_id=1, source_target_pairs={{0,8},{8,16},{16,24},{24,32},{32,40},{40,48},{48,56},{56,64},{64,7... | collective-permute-start | bytes 491528 | tf_op jit(solution)/shard_map/while/body/eval_jaxpr/ppermute | solution.py:17
  (74 other events, 428.0 us)
Sparse Core Ops, SparseCore 0:
  10.6 38.4 all-gather.10
  51.3 34.8 all-gather.6
  88.0 34.8 all-gather.12
  124.5 34.8 all-gather.8
  266.8 91.8 all-reduce.2
  430.9 46.5 all-gather.14
  488.9 119.1 reduce-scatter.1
where the time goes:
time: 715 us; the launch traced here: 706 us
  waiting for transfers between devices  386 us (54%)
  matrix products  84.5 us (12%)
  blocking collectives  67.5 us (9%)
  local copies, waits for them, and re-layouts  54.6 us (8%)
  starting transfers between devices  53.3 us (7%)
  other arithmetic  41.7 us (6%)
  between operations  15.7 us (2%)
    ppermute x64, waiting for transfers between devices, shifted(): lax.ppermute(value, axis, [(i, (i + by) % count) for i in range(count)])  105 us
    unnamed x8, waiting for transfers between devices  91.2 us
    psum x1, blocking collectives, on_device(): square_sum = lax.psum(jnp.sum(target * target), ('seq', 'tp'))  67.5 us
    ppermute x64, starting transfers between devices, shifted(): lax.ppermute(value, axis, [(i, (i + by) % count) for i in range(count)])  52.8 us
    all_gather x1, waiting for transfers between devices, on_device(): piece = lax.all_gather(cotangent, 'tp', axis=0, tiled=True)  46.6 us
    all_gather x1, waiting for transfers between devices, on_device(): lax.all_gather(key_proj, 'seq', axis=0, tiled=True)  37.2 us
    all_gather x1, waiting for transfers between devices, on_device(): lax.all_gather(value_tan, 'seq', axis=0, tiled=True)  36.6 us
    all_gather x1, waiting for transfers between devices, on_device(): lax.all_gather(key_tan, 'seq', axis=0, tiled=True)  36.5 us
  transfers between devices with their start and end apart: 71, of which 38 were waited for; matrix products, arithmetic and copies ran while one was open for 8% of the time, Pallas kernels for 0%

commit v1 on v0

v1 whole, which is shorter than its diff:
```python
import math

import jax
import jax.numpy as jnp
from jax import lax
from jax.experimental import pallas as pl
from jax.experimental.pallas import tpu as pltpu
from jax.sharding import PartitionSpec as P

HD = 128
TSTEPS = 64
FRAMES = 16
ROWS = 160
UNIT = 320
NCHIP = 8
NQ = 640
SCALE = 1.0 / math.sqrt(HD)
MESH = pl.DeviceIdType.MESH
F32 = jnp.float32
BF16 = jnp.bfloat16


def dot_nt(a, b):
    return lax.dot_general(a, b, (((1,), (1,)), ((), ())), preferred_element_type=F32)


def dot_nn(a, b):
    return lax.dot_general(a, b, (((1,), (0,)), ((), ())), preferred_element_type=F32)


def dot_tn(a, b):
    return lax.dot_general(a, b, (((0,), (0,)), ((), ())), preferred_element_type=F32)


def kernel(
    frame_ref,
    time_ref,
    q_ref,
    k_ref,
    v_ref,
    qd_ref,
    kd_ref,
    vd_ref,
    w_hbm,
    noisy_ref,
    vel_ref,
    dq_out,
    dk_out,
    dv_out,
    gw_out,
    ms_out,
    w,
    kk,
    vv,
    qq,
    sbuf,
    stbuf,
    p16,
    acc1,
    acc2,
    ublk,
    uown,
    at_own,
    at,
    negb,
    part,
    rs_rx,
    cot,
    g_tx,
    g,
    dqt,
    dq_tx,
    dq_rx,
    dkv,
    sib_rx,
    dkv_tx,
    dkv_rx,
    tw,
    sq_tp,
    sq_seq,
    wsem,
    kv_send,
    kv_recv,
    fw_send,
    fw_recv,
    q_send,
    q_recv,
    u_send,
    u_recv,
    at_send,
    at_recv,
    atf_send,
    atf_recv,
    rs_send,
    rs_recv,
    t_send,
    t_recv,
    g_send,
    g_recv,
    tw_send,
    tw_recv,
    dq_send,
    dq_recv,
    sib_send,
    sib_recv,
    dkv_send,
    dkv_recv,
    sqt_send,
    sqt_recv,
    sqs_send,
    sqs_recv,
):
    s = lax.axis_index("seq")
    t = lax.axis_index("tp")
    x = s // 4
    y = (s // 2) % 2
    c = s % 2
    m = s // 2
    yh = t // 4
    z = t % 4
    j = s % 4
    head = x

    chips = [(dx, dy) for dx in (2, 1, 3, 0) for dy in (1, 0)]
    far_chips = [d for d in chips if d != (0, 0)]
    tps = [(a, b) for a in (1, 0) for b in (2, 1, 3, 0) if a or b]

    def chip_at(dx, dy):
        return lax.rem(x + dx, 4), lax.rem(y + dy, 2)

    def chip_dev(dx, dy):
        cx, cy = chip_at(dx, dy)
        return cx * 4 + cy * 2 + c

    def tp_at(dyh, dz):
        return lax.rem(yh + dyh, 2) * 4 + lax.rem(z + dz, 4)

    def tp_from(dyh, dz):
        return lax.rem(yh + 2 - dyh, 2) * 4 + lax.rem(z + 4 - dz, 4)

    def remote(src, dst, ssem, rsem, dev):
        return pltpu.make_async_remote_copy(
            src_ref=src, dst_ref=dst, send_sem=ssem, recv_sem=rsem, device_id=dev, device_id_type=MESH
        )

    def lanes(index, width):
        return pl.ds(pl.multiple_of(index * width, width), width)

    def wait_for(ref, sem):
        pltpu.make_async_copy(ref, ref, sem).wait()

    wload = pltpu.make_async_copy(w_hbm, w, wsem)
    wload.start()

    barrier = pltpu.get_barrier_semaphore()
    sibling = s + 1 - 2 * c
    for d in range(1, 16):
        pl.semaphore_signal(barrier, inc=1, device_id=(lax.rem(s + d, 16), t), device_id_type=MESH)
    for dyh, dz in tps:
        pl.semaphore_signal(barrier, inc=1, device_id=(s, tp_at(dyh, dz)), device_id_type=MESH)
    pl.semaphore_wait(barrier, 22)

    kv_src = (k_ref, kd_ref, v_ref, vd_ref)
    kv_dst = ((kk, 0), (kk, 1), (vv, 0), (vv, 1))

    def kv_copy(a, i, dx, dy):
        hx, hy = chip_at(dx, dy)
        buf, half = kv_dst[a]
        return remote(
            kv_src[a].at[:, lanes(hx, HD)],
            buf.at[m, c, :, half * HD : (half + 1) * HD],
            kv_send.at[a, i],
            kv_recv.at[a],
            (hx * 4 + hy * 2 + c, t),
        )

    def kv_local(a):
        buf, half = kv_dst[a]
        return pltpu.make_async_copy(
            kv_src[a].at[:, lanes(x, HD)],
            buf.at[m, c, :, half * HD : (half + 1) * HD],
            kv_recv.at[a],
        )

    def to_heads(src_of, dst, send, recv, slot, act):
        qj = jnp.where(m < 4, m, 7 - m)
        qu = m // 4
        for dx in range(4):
            hx = lax.rem(x + dx, 4)
            dev = hx * 4 + qj
            if dx:
                copy = remote(src_of(hx), dst(qu), send.at[slot, dx], recv, (dev, t))
                copy.start() if act == "start" else copy.wait_send()
            else:

                @pl.when(dev != s)
                def _():
                    copy = remote(src_of(hx), dst(qu), send.at[slot, dx], recv, (dev, t))
                    copy.start() if act == "start" else copy.wait_send()

                if act == "start":

                    @pl.when(dev == s)
                    def _():
                        pltpu.make_async_copy(src_of(hx), dst(qu), recv).start()

    def to_owners(src, dst, send, recv, act):
        for u in range(2):
            um = j if u == 0 else 7 - j
            for core in range(2):
                dev = um * 2 + core

                @pl.when(dev != s)
                def _():
                    copy = remote(src.at[u, core], dst, send.at[u, core], recv, (dev, t))
                    copy.start() if act == "start" else copy.wait_send()

                if act == "start":

                    @pl.when(dev == s)
                    def _():
                        pltpu.make_async_copy(src.at[u, core], dst, recv).start()

    def q_moves(act):
        for a, ref in ((1, q_ref), (0, qd_ref)):
            to_heads(
                lambda hx, ref=ref: ref.at[:, lanes(hx, HD)],
                lambda qu, a=a: qq.at[qu, c, :, a * HD : (a + 1) * HD],
                q_send,
                q_recv,
                a,
                act,
            )

    def kv_start(a):
        kv_local(a).start()
        for i, (dx, dy) in enumerate(far_chips):
            kv_copy(a, i, dx, dy).start()

    kv_start(0)
    q_moves("start")
    kv_start(1)
    kv_start(2)
    kv_start(3)

    ends = []
    total = 0
    for f in range(FRAMES):
        total = total + frame_ref[f]
        ends.append(total)
    times = [time_ref[f] for f in range(FRAMES)]

    def frame_facts(pos):
        kend = jnp.zeros(pos.shape, jnp.int32) + ends[FRAMES - 1]
        level = jnp.zeros(pos.shape, jnp.int32) + times[FRAMES - 1]
        for f in range(FRAMES - 2, -1, -1):
            inside = pos < ends[f]
            kend = jnp.where(inside, ends[f], kend)
            level = jnp.where(inside, times[f], level)
        angle = (level.astype(F32) + 0.5) * (math.pi / (2 * TSTEPS))
        return kend, jnp.cos(angle), jnp.sin(angle)

    lane = lax.broadcasted_iota(jnp.int32, (1, NQ), 1)
    qpos = jnp.where(lane < UNIT, UNIT * j + lane, UNIT * (7 - j) + lane - UNIT)
    kend, cosq, sinq = frame_facts(qpos)

    rpos = s * ROWS + t * 20 + lax.broadcasted_iota(jnp.int32, (20, 1), 0)
    _, cosr, sinr = frame_facts(rpos)
    negb[...] = jnp.zeros_like(negb)
    negb[0:20, :] = sinr * cosr * noisy_ref[...].astype(F32) - cosr * cosr * vel_ref[...].astype(F32)

    def fw_copy(a):
        buf, half = kv_dst[a]
        view = buf.at[:, c, :, half * HD : (half + 1) * HD]
        return remote(view, view, fw_send.at[a], fw_recv.at[a], (sibling, t))

    def kv_forward(a):
        buf, half = kv_dst[a]
        wait_for(buf.at[:, c, :, half * HD : (half + 1) * HD], kv_recv.at[a])
        fw_copy(a).start()

    def kv_arrived(a):
        fw_copy(a).wait_recv()

    n0 = j + 2
    n1 = jnp.minimum(9 - j, 8)

    def over_keys(body, carry):
        carry = lax.fori_loop(0, n0, lambda i, st: body(i, st, 0), carry)
        return lax.fori_loop(n0, n1, lambda i, st: body(i, st, 256), carry)

    def put(row, lo, part_row):
        if lo == 0:
            return part_row
        return jnp.concatenate([row[:, :lo], part_row], axis=1)

    kv_forward(0)
    wait_for(qq, q_recv)
    kv_arrived(0)

    def chunk(buf, i):
        return buf[i].reshape(UNIT, buf.shape[-1])

    def pass1(i, top, lo):
        keys = kk[i, :, :, :HD].reshape(UNIT, HD)
        queries = qq[...].reshape(NQ, 2 * HD)[lo:, HD:]
        sc = dot_nt(keys, queries) * SCALE
        kpos = i * UNIT + lax.broadcasted_iota(jnp.int32, (UNIT, 1), 0)
        sc = jnp.where(kpos < kend[:, lo:], sc, -1e30)
        sbuf[i, :, lo:] = sc
        return put(top, lo, jnp.maximum(top[:, lo:], jnp.max(sc, axis=0, keepdims=True)))

    top = over_keys(pass1, jnp.full((1, NQ), -1e30, F32))

    kv_forward(1)
    kv_forward(2)
    kv_forward(3)
    kv_arrived(1)

    def pass2(i, state, lo):
        den, tan = state
        st = dot_nt(chunk(kk, i), qq[...].reshape(NQ, 2 * HD)[lo:]) * SCALE
        p = jnp.exp(sbuf[i, :, lo:] - top[:, lo:])
        sbuf[i, :, lo:] = p
        stbuf[i, :, lo:] = st
        den = put(den, lo, den[:, lo:] + jnp.sum(p, axis=0, keepdims=True))
        tan = put(tan, lo, tan[:, lo:] + jnp.sum(p * st, axis=0, keepdims=True))
        return den, tan

    row0 = jnp.zeros((1, NQ), F32)
    den, tan = over_keys(pass2, (row0, row0))
    inv = 1.0 / den
    mean = tan * inv
    kv_arrived(2)
    kv_arrived(3)

    acc1[...] = jnp.zeros_like(acc1)
    acc2[...] = jnp.zeros_like(acc2)

    def pass3(i, state, lo):
        p = sbuf[i, :, lo:] * inv[:, lo:]
        ph = p.astype(BF16)
        p16[i, :, lo:] = ph
        ds = (p * (stbuf[i, :, lo:] - mean[:, lo:])).astype(BF16)
        vals = chunk(vv, i)
        acc1[:, lo:] += dot_tn(vals, ph)
        acc2[:, lo:] += dot_tn(vals[:, :HD], ds)
        return state

    over_keys(pass3, 0)
    attn_t = acc1[0:HD, :].astype(BF16)
    tan_t = (acc2[...] + acc1[HD:, :]).astype(BF16)
    at_own[...] = attn_t
    u_t = (0.5 * cosq) * (cosq * attn_t.astype(F32) + sinq * tan_t.astype(F32))
    ublk[...] = u_t.T.astype(BF16).reshape(2, 2, ROWS, HD)
    to_owners(ublk, uown.at[:, lanes(head, HD)], u_send, u_recv, "start")

    def at_copy(i, dx, dy):
        return remote(
            at_own, at.at[y, c, lanes(head, HD), :], at_send.at[i], at_recv, (chip_dev(dx, dy), t)
        )

    pltpu.make_async_copy(at_own, at.at[y, c, lanes(head, HD), :], at_recv).start()
    for i, (dx, dy) in enumerate(far_chips):
        at_copy(i, dx, dy).start()

    wload.wait()
    wait_for(uown, u_recv)
    u = uown[...]
    pick = (
        lax.broadcasted_iota(jnp.int32, (ROWS, 32), 0)
        == t * 20 + lax.broadcasted_iota(jnp.int32, (ROWS, 32), 1)
    ) & (lax.broadcasted_iota(jnp.int32, (ROWS, 32), 1) < 20)
    pick = pick.astype(F32).astype(BF16)

    def partial(tt):
        return dot_nn(u, w[:, lanes(tt, 512)]) + dot_nn(pick, negb[:, lanes(tt, 512)].astype(BF16))

    def rs_copy(dyh, dz):
        slot = dyh * 4 + dz
        return remote(
            part.at[slot], rs_rx.at[slot], rs_send.at[slot], rs_recv.at[slot], (s, tp_at(dyh, dz))
        )

    for dyh, dz in tps:
        part[dyh * 4 + dz] = partial(tp_at(dyh, dz)).astype(BF16)
        rs_copy(dyh, dz).start()
    total = partial(t)
    for dyh, dz in reversed(tps):
        rs_copy(dyh, dz).wait_recv()
        total = total + rs_rx[dyh * 4 + dz].astype(F32)
    cot[0] = total.astype(BF16)

    def t_copy(dyh, dz):
        slot = dyh * 4 + dz
        return remote(
            cot.at[0], cot.at[slot], t_send.at[slot], t_recv.at[slot], (s, tp_at(dyh, dz))
        )

    for dyh, dz in tps:
        t_copy(dyh, dz).start()

    def sqt_copy(dyh, dz):
        slot = dyh * 4 + dz
        return remote(
            sq_tp.at[0], sq_tp.at[slot], sqt_send.at[slot], sqt_recv.at[slot], (s, tp_at(dyh, dz))
        )

    sq = jnp.sum(jnp.sum(total * total, axis=0, keepdims=True), axis=1, keepdims=True)
    sq_tp[0] = jnp.zeros((8, 128), F32) + sq
    for dyh, dz in tps:
        sqt_copy(dyh, dz).start()

    grad = dot_nt(cot[0], w[:, lanes(t, 512)])
    for dyh, dz in reversed(tps):
        t_copy(dyh, dz).wait_recv()
        grad = grad + dot_nt(cot[dyh * 4 + dz], w[:, lanes(tp_from(dyh, dz), 512)])
    g_tx[...] = grad.astype(BF16)

    def g_moves(act):
        to_heads(
            lambda hx: g_tx.at[:, lanes(hx, HD)],
            lambda qu: g.at[qu, c],
            g_send,
            g_recv,
            0,
            act,
        )

    g_moves("start")

    sqv = sq_tp[0]
    for dyh, dz in tps:
        sqt_copy(dyh, dz).wait_recv()
        sqv = sqv + sq_tp[dyh * 4 + dz]
    sq_seq[0] = sqv

    def sqs_copy(d):
        return remote(
            sq_seq.at[0], sq_seq.at[d], sqs_send.at[d], sqs_recv.at[d], (lax.rem(s + d, 16), t)
        )

    for d in range(1, 16):
        sqs_copy(d).start()

    def tw_slot(src):
        sm = src // 2
        return jnp.where(sm < 4, sm, 7 - sm), sm // 4, src % 2

    def tw_view():
        a, b, e = tw_slot(s)
        return tw.at[a, b, e]

    def tw_src(dest):
        tt = dest // 2
        slot = lax.rem(yh + 2 - tt // 4, 2) * 4 + lax.rem(z + 4 - tt % 4, 4)
        return cot.at[slot, :, lanes(dest % 2, 256)]

    def tw_copy(d):
        dest = lax.rem(s + d, 16)
        return remote(tw_src(dest), tw_view(), tw_send.at[d], tw_recv, (dest, t))

    for d in range(1, 16):
        tw_copy(d).start()
    pltpu.make_async_copy(tw_src(s), tw_view(), tw_recv).start()

    wait_for(g, g_recv)
    gt = g[...].reshape(NQ, HD).astype(F32).T
    dterm = jnp.sum(gt * at_own[...].astype(F32), axis=0, keepdims=True)
    dqt[...] = jnp.zeros_like(dqt)

    def zero(i, state):
        dkv[:, i] = jnp.zeros((2, 2, ROWS, HD), BF16)
        return state

    lax.fori_loop(n1, 8, zero, 0)

    def back(i, state, lo):
        gq = g[...].reshape(NQ, HD)[lo:]
        queries = qq[...].reshape(NQ, 2 * HD)[lo:, HD:]
        keys = chunk(kk, i)[:, :HD]
        vals = chunk(vv, i)[:, :HD]
        ph = p16[i, :, lo:]
        dp = dot_nt(vals, gq)
        ds = (ph.astype(F32) * (dp - dterm[:, lo:])).astype(BF16)
        dkv[1, i] = dot_nn(ph, gq).astype(BF16).reshape(2, ROWS, HD)
        dkv[0, i] = (dot_nn(ds, queries) * SCALE).astype(BF16).reshape(2, ROWS, HD)
        dqt[:, lo:] += dot_tn(keys, ds)
        return state

    over_keys(back, 0)

    sib = remote(dkv.at[:, :, 1 - c], sib_rx, sib_send, sib_recv, (sibling, t))
    sib.start()
    dq_tx[...] = (dqt[...] * SCALE).T.astype(BF16).reshape(2, 2, ROWS, HD)
    to_owners(dq_tx, dq_rx.at[:, lanes(head, HD)], dq_send, dq_recv, "start")
    sib.wait_recv()
    dkv_tx[...] = (dkv[:, :, c].astype(F32) + sib_rx[...].astype(F32)).astype(BF16)

    def dkv_copy(dx, dy):
        cx, cy = chip_at(dx, dy)
        slot = dx * 2 + dy
        return remote(
            dkv_tx.at[:, cx * 2 + cy],
            dkv_rx.at[slot],
            dkv_send.at[slot],
            dkv_recv.at[slot],
            (chip_dev(dx, dy), t),
        )

    for dx, dy in far_chips:
        dkv_copy(dx, dy).start()

    wait_for(at.at[:, c], at_recv)
    atf = remote(at.at[:, c], at.at[:, c], atf_send, atf_recv, (sibling, t))
    atf.start()
    wait_for(tw, tw_recv)
    atf.wait_recv()

    gw = dot_nn(at[0, 0], tw[0].reshape(NQ, 256))
    for a in range(1, 4):
        gw = gw + dot_nn(at[a // 2, a % 2], tw[a].reshape(NQ, 256))
    gw_out[...] = gw

    sqv = sq_seq[0]
    for d in range(1, 16):
        sqs_copy(d).wait_recv()
        sqv = sqv + sq_seq[d]
    ms_out[...] = sqv

    wait_for(dq_rx, dq_recv)
    dq_out[...] = dq_rx[...]

    for dx in range(4):
        hx = lax.rem(x + 4 - dx, 4)
        tot = [None, None]
        for dy in (0, 1):
            if dx or dy:
                dkv_copy(dx, dy).wait_recv()
            for a in range(2):
                piece = dkv_rx[dx * 2 + dy, a] if dx or dy else dkv_tx[a, m]
                piece = piece.astype(F32)
                tot[a] = piece if tot[a] is None else tot[a] + piece
        dk_out[:, lanes(hx, HD)] = tot[0]
        dv_out[:, lanes(hx, HD)] = tot[1]

    for a in range(4):
        for i, (dx, dy) in enumerate(far_chips):
            kv_copy(a, i, dx, dy).wait_send()
        fw_copy(a).wait_send()
    q_moves("wait")
    to_owners(ublk, uown.at[:, lanes(head, HD)], u_send, u_recv, "wait")
    for i, (dx, dy) in enumerate(far_chips):
        at_copy(i, dx, dy).wait_send()
        dkv_copy(dx, dy).wait_send()
    for dyh, dz in tps:
        rs_copy(dyh, dz).wait_send()
        t_copy(dyh, dz).wait_send()
        sqt_copy(dyh, dz).wait_send()
    g_moves("wait")
    for d in range(1, 16):
        sqs_copy(d).wait_send()
        tw_copy(d).wait_send()
    sib.wait_send()
    to_owners(dq_tx, dq_rx.at[:, lanes(head, HD)], dq_send, dq_recv, "wait")
    atf.wait_send()


def on_device(q, k, v, qd, kd, vd, w, noisy, vel, time_index, frame_lengths):
    smem = pl.BlockSpec(memory_space=pltpu.SMEM)
    vmem = pl.BlockSpec(memory_space=pltpu.VMEM)
    hbm = pl.BlockSpec(memory_space=pl.ANY)
    dma = pltpu.SemaphoreType.DMA
    scratch = [
        pltpu.VMEM((512, 4096), BF16),
        pltpu.VMEM((NCHIP, 2, ROWS, 256), BF16),
        pltpu.VMEM((NCHIP, 2, ROWS, 256), BF16),
        pltpu.VMEM((2, 2, ROWS, 256), BF16),
        pltpu.VMEM((NCHIP, UNIT, NQ), F32),
        pltpu.VMEM((NCHIP, UNIT, NQ), F32),
        pltpu.VMEM((NCHIP, UNIT, NQ), BF16),
        pltpu.VMEM((256, NQ), F32),
        pltpu.VMEM((128, NQ), F32),
        pltpu.VMEM((2, 2, ROWS, HD), BF16),
        pltpu.VMEM((ROWS, 512), BF16),
        pltpu.VMEM((HD, NQ), BF16),
        pltpu.VMEM((2, 2, 512, NQ), BF16),
        pltpu.VMEM((32, 4096), F32),
        pltpu.VMEM((8, ROWS, 512), BF16),
        pltpu.VMEM((8, ROWS, 512), BF16),
        pltpu.VMEM((8, ROWS, 512), BF16),
        pltpu.VMEM((ROWS, 512), BF16),
        pltpu.VMEM((2, 2, ROWS, HD), BF16),
        pltpu.VMEM((HD, NQ), F32),
        pltpu.VMEM((2, 2, ROWS, HD), BF16),
        pltpu.VMEM((ROWS, 512), BF16),
        pltpu.VMEM((2, NCHIP, 2, ROWS, HD), BF16),
        pltpu.VMEM((2, NCHIP, ROWS, HD), BF16),
        pltpu.VMEM((2, NCHIP, ROWS, HD), BF16),
        pltpu.VMEM((NCHIP, 2, ROWS, HD), BF16),
        pltpu.VMEM((4, 2, 2, ROWS, 256), BF16),
        pltpu.VMEM((8, 8, 128), F32),
        pltpu.VMEM((16, 8, 128), F32),
        dma,
        dma((4, 7)),
        dma((4,)),
        dma((4,)),
        dma((4,)),
        dma((2, 4)),
        dma,
        dma((2, 2)),
        dma,
        dma((7,)),
        dma,
        dma,
        dma,
        dma((8,)),
        dma((8,)),
        dma((8,)),
        dma((8,)),
        dma((1, 4)),
        dma,
        dma((16,)),
        dma,
        dma((2, 2)),
        dma,
        dma,
        dma,
        dma((8,)),
        dma((8,)),
        dma((8,)),
        dma((8,)),
        dma((16,)),
        dma((16,)),
    ]
    dq, dk, dv, gw, ms = pl.pallas_call(
        kernel,
        out_shape=(
            jax.ShapeDtypeStruct((ROWS, 512), BF16),
            jax.ShapeDtypeStruct((ROWS, 512), F32),
            jax.ShapeDtypeStruct((ROWS, 512), F32),
            jax.ShapeDtypeStruct((512, 256), F32),
            jax.ShapeDtypeStruct((8, 128), F32),
        ),
        in_specs=[smem, smem] + [hbm] * 7 + [vmem] * 2,
        out_specs=(vmem,) * 5,
        scratch_shapes=scratch,
        compiler_params=pltpu.CompilerParams(
            collective_id=0, has_side_effects=True, vmem_limit_bytes=56 * 1024 * 1024
        ),
        cost_estimate=pl.CostEstimate(flops=7 * 10**9, bytes_accessed=8 * 10**6, transcendentals=1638400),
    )(frame_lengths, time_index, q, k, v, qd, kd, vd, w, noisy, vel)
    scale = lax.rsqrt(ms[0, 0] / (2560 * 4096) + 1e-05)
    return tuple((part.astype(F32) * scale).astype(BF16) for part in (dq, dk, dv, gw))


def solution(mesh):
    in_specs = (P("seq", "tp"),) * 6 + (P("tp", None), P(("seq", "tp"), None), P(("seq", "tp"), None), P(), P())
    out_specs = (P("seq", "tp"), P("seq", "tp"), P("seq", "tp"), P("tp", "seq"))
    return jax.shard_map(
        on_device, mesh=mesh, in_specs=in_specs, out_specs=out_specs, check_vma=False
    )
```

time: 715 us -> 128 us (0.18); the launches traced: 706 us -> 128 us
  waiting for transfers between devices: 386 us -> 0 us
  Pallas kernels: 0 us -> 120 us
  matrix products: 84.5 us -> 0 us
  blocking collectives: 67.5 us -> 0 us
  local copies, waits for them, and re-layouts: 54.6 us -> 1.19 us
  starting transfers between devices: 53.3 us -> 0 us
  other arithmetic: 41.7 us -> 5.24 us
  between operations: 15.7 us -> 1.34 us
    all_gather x5 -> x0, waiting for transfers between devices: 190 us -> none  [the longest x1 46.6 us: on_device(): piece = lax.all_gather(cotangent, 'tp', axis=0, tiled=True)]
    pallas_call x0 -> x1, Pallas kernels: none -> 120 us  [on_device(): pl.pallas_call(kernel, out_shape=(jax.ShapeDtypeStruct((ROWS, 512), BF16)...]
    ppermute x64 -> x0, waiting for transfers between devices: 105 us -> none  [shifted(): lax.ppermute(value, axis, [(i, (i + by) % count) for i in range(count)])]
    unnamed x8 -> x0, waiting for transfers between devices: 91.2 us -> none
    dot_general x107 -> x0, matrix products: 84.5 us -> none  [the longest x4 12.4 us: forward_step(): jnp.einsum('hqk,khd->hqd', weights, values_dot_wide, precision=highest, p...]
    psum x1 -> x0, blocking collectives: 67.5 us -> none  [on_device(): square_sum = lax.psum(jnp.sum(target * target), ('seq', 'tp'))]
    ppermute x64 -> x0, starting transfers between devices: 52.8 us -> none  [shifted(): lax.ppermute(value, axis, [(i, (i + by) % count) for i in range(count)])]
    dynamic_slice x24 -> x0, local copies, waits for them, and re-layouts: 35.4 us -> none  [loop_step(): lax.dynamic_slice_in_dim(member, offset, block_rows, 0)]
  transfers between devices with their start and end apart: 71 -> 0, of which waited for: 38 -> 0; matrix products, arithmetic and copies ran while one was open for 8% -> 0% of each run, Pallas kernels for 0% -> 0%
where the time goes in v1:
time: 128 us
  Pallas kernels  120 us (94%)
  other arithmetic  5.24 us (4%)
  between operations  1.34 us (1%)
    pallas_call x1, Pallas kernels, on_device(): pl.pallas_call(kernel, out_shape=(jax.ShapeDtypeStruct((ROWS, 512), BF16)...  120 us
    convert_element_type x3, other arithmetic, on_device(): (part.astype(F32) * scale).astype(BF16)  5.24 us

profile of v1, /device:TPU:1, one launch (start us, length us, event | category | flops | bytes accessed | tf_op | source)
XLA Modules:
  0.0 127.5 jit_solution(10089434887849422867)
XLA Ops:
  0.6 119.8 %shard_map.138 = (bf16[160,512]{1,0:T(8,128)(2,1)}, f32[160,512]{1,0:T(8,128)}, f32[160,512]{1,0:T(8,128)}, f32[512,256]{1,0:T(8,128)}, f32[8,128]{1,0:T(8,128)}) custom-call(s32[16]{0:T(128)} %frame_ref.1, s32[16]{0:T(128)} %time_ref.1, bf16[160,512]{1,0:T(8,128)(2,1)} %q_ref.1, bf16[160,512]{1,0:T(8,128)(2,1)} %k_ref.1, bf16[160,512]{1,0:T(8,128)(2,1)} %v_ref.1, ...), custom_call_target="tpu_custom_call" | custom-call | flops 7000000000 | bytes 8000000 | tf_op jit(solution)/shard_map/pallas_call | solution.py:636
  120.4 1.2 slice.3
  122.3 1.6 %multiply_convert_fusion.3 = bf16[160,512]{1,0:T(8,128)(2,1)} fusion(bf16[160,512]{1,0:T(8,128)(2,1)} %get-tuple-element.9, f32[]{:T(128)} %bitcast), kind=kLoop, calls=%fused_computation.3 | loop fusion | flops 245760 | bytes 327684 | tf_op jit(solution)/shard_map/convert_element_type | solution.py:654
  123.9 1.8 %multiply_convert_fusion = bf16[512,256]{1,0:T(8,128)(2,1)} fusion(f32[512,256]{1,0:T(8,128)} %get-tuple-element.13, f32[]{:T(128)} %bitcast), kind=kLoop, calls=%fused_computation | loop fusion | flops 262144 | bytes 786436 | tf_op jit(solution)/shard_map/convert_element_type | solution.py:654
  125.7 1.8 %multiply_convert_fusion.1 = (bf16[160,512]{1,0:T(8,128)(2,1)}, bf16[160,512]{1,0:T(8,128)(2,1)}) fusion(f32[160,512]{1,0:T(8,128)} %get-tuple-element.12, f32[]{:T(128)} %bitcast, f32[160,512]{1,0:T(8,128)} %get-tuple-element.11), kind=kLoop, calls=%fused_computation.1 | loop fusion | flops 327680 | bytes 983044 | tf_op jit(solution)/shard_map/convert_element_type | solution.py:654

commit v2 on v1

v2 whole, which is shorter than its diff:
```python
import math

import jax
import jax.numpy as jnp
from jax import lax
from jax.experimental import pallas as pl
from jax.experimental.pallas import tpu as pltpu
from jax.sharding import PartitionSpec as P

HD = 128
TSTEPS = 64
FRAMES = 16
ROWS = 160
UNIT = 320
NCHIP = 8
NQ = 640
SCALE = 1.0 / math.sqrt(HD)
MESH = pl.DeviceIdType.MESH
F32 = jnp.float32
BF16 = jnp.bfloat16


def dot_nt(a, b):
    return lax.dot_general(a, b, (((1,), (1,)), ((), ())), preferred_element_type=F32)


def dot_nn(a, b):
    return lax.dot_general(a, b, (((1,), (0,)), ((), ())), preferred_element_type=F32)


def dot_tn(a, b):
    return lax.dot_general(a, b, (((0,), (0,)), ((), ())), preferred_element_type=F32)


def kernel(
    frame_ref,
    time_ref,
    q_ref,
    k_ref,
    v_ref,
    qd_ref,
    kd_ref,
    vd_ref,
    w_hbm,
    noisy_ref,
    vel_ref,
    dq_out,
    dk_out,
    dv_out,
    gw_out,
    ms_out,
    w,
    kk,
    vv,
    qq,
    sbuf,
    stbuf,
    p16,
    acc1,
    acc2,
    ublk,
    uown,
    at_own,
    at,
    negb,
    part_a,
    part_b,
    rx_a,
    rx_b,
    sum_a,
    sum_b,
    part_a2,
    part_b2,
    rx_a2,
    rx_b2,
    cot,
    g_tx,
    g,
    dqt,
    dq_tx,
    dq_rx,
    dkv,
    sib_rx,
    dkv_tx,
    dkv_rx,
    tw_part,
    tw,
    sq_tp,
    sq_seq,
    wsem,
    kvx_send,
    kvx_recv,
    kvy_send,
    kvy_recv,
    fwx_send,
    fwx_recv,
    fwy_send,
    fwy_recv,
    q_send,
    q_recv,
    u_send,
    u_recv,
    atx_send,
    atx_recv,
    aty_send,
    aty_recv,
    at2_recv,
    atf_send,
    atf_recv,
    rsa_send,
    rsa_recv,
    rsb_send,
    rsb_recv,
    rsa2_send,
    rsa2_recv,
    rsb2_send,
    rsb2_recv,
    t_send,
    t_recv,
    g_send,
    g_recv,
    tw_send,
    tw_recv,
    twg_send,
    twg_recv,
    dq_send,
    dq_recv,
    sib_send,
    sib_recv,
    dkv_send,
    dkv_recv,
    sqt_send,
    sqt_recv,
    sqs_send,
    sqs_recv,
):
    s = lax.axis_index("seq")
    t = lax.axis_index("tp")
    x = s // 4
    y = (s // 2) % 2
    c = s % 2
    m = s // 2
    yh = t // 4
    z = t % 4
    head = x
    far = (2, 1, 3)

    def ring(pos, step):
        return lax.rem(pos + step, 4)

    def seq_dev(px, py, pc):
        return (px * 4 + py * 2 + pc, t)

    def tp_dev(pyh, pz):
        return (s, pyh * 4 + pz)

    def remote(src, dst, ssem, rsem, dev):
        return pltpu.make_async_remote_copy(
            src_ref=src, dst_ref=dst, send_sem=ssem, recv_sem=rsem, device_id=dev, device_id_type=MESH
        )

    def lanes(index, width):
        return pl.ds(pl.multiple_of(index * width, width), width)

    def wait_for(ref, sem):
        pltpu.make_async_copy(ref, ref, sem).wait()

    pending = []

    def launch(copy):
        copy.start()
        pending.append(copy.wait_send)

    owed = {}

    def due(name):
        owed.pop(name)()

    def finish():
        for name in list(owed):
            due(name)
        for wait in pending:
            wait()

    wload = pltpu.make_async_copy(w_hbm, w, wsem)
    wload.start()
    owed["w"] = wload.wait

    barrier = pltpu.get_barrier_semaphore()
    sibling = s + 1 - 2 * c
    for d in range(1, 16):
        pl.semaphore_signal(barrier, inc=1, device_id=(lax.rem(s + d, 16), t), device_id_type=MESH)
    for d in range(1, 8):
        pl.semaphore_signal(barrier, inc=1, device_id=(s, lax.rem(t + d, 8)), device_id_type=MESH)
    pl.semaphore_wait(barrier, 22)

    kv_src = (k_ref, kd_ref, v_ref, vd_ref)
    kv_dst = ((kk, 0), (kk, 1), (vv, 0), (vv, 1))

    def kv_view(a, px, py, pc):
        buf, half = kv_dst[a]
        return buf.at[px, py, pc, :, half * HD : (half + 1) * HD]

    def kv_piece(a, px):
        return kv_src[a].at[:, lanes(px, HD)]

    def kv_all(a, py, pc):
        return kv_view(a, slice(None), py, pc)

    def kv_own(a):
        pltpu.make_async_copy(kv_piece(a, x), kv_view(a, x, y, c), kvx_recv.at[a]).start()
        launch(
            remote(
                kv_piece(a, x), kv_view(a, x, y, c), kvy_send.at[a, 0], kvy_recv.at[a], seq_dev(x, 1 - y, c)
            )
        )

    def kv_along_x(a):
        for dx in far:
            hx = ring(x, dx)
            launch(
                remote(
                    kv_piece(a, hx), kv_view(a, x, y, c), kvx_send.at[a, dx], kvx_recv.at[a], seq_dev(hx, y, c)
                )
            )
        owed["kvx", a] = lambda: wait_for(kv_all(a, y, c), kvx_recv.at[a])
        owed["kvy", a] = lambda: wait_for(kv_all(a, 1 - y, c), kvy_recv.at[a])

    def kv_across(a):
        due(("kvx", a))
        for dx in far:
            view = kv_view(a, ring(x, dx), y, c)
            launch(remote(view, view, kvy_send.at[a, dx], kvy_recv.at[a], seq_dev(x, 1 - y, c)))
        to_sibling(a, y, fwx_send, fwx_recv, "fwx")

    def to_sibling(a, py, send, recv, name):
        view = kv_all(a, py, c)
        launch(remote(view, view, send.at[a], recv.at[a], (sibling, t)))
        owed[name, a] = lambda: wait_for(kv_all(a, py, 1 - c), recv.at[a])

    def kv_received(a):
        due(("kvy", a))
        to_sibling(a, 1 - y, fwy_send, fwy_recv, "fwy")

    def kv_complete(a):
        due(("fwx", a))
        due(("fwy", a))

    home = jnp.where((x == 1) | (x == 2), 1, 0)
    unit = x // 2

    def to_heads(src_of, dst, send, recv, slot, act):
        for dx in (2, 1, 3, 0):
            hx = ring(x, dx)
            if dx:
                copy = remote(src_of(hx), dst, send.at[slot, dx], recv, seq_dev(hx, y, home))
                copy.start() if act == "start" else copy.wait_send()
            else:

                @pl.when(home != c)
                def _():
                    copy = remote(src_of(hx), dst, send.at[slot, dx], recv, seq_dev(hx, y, home))
                    copy.start() if act == "start" else copy.wait_send()

                if act == "start":

                    @pl.when(home == c)
                    def _():
                        pltpu.make_async_copy(src_of(hx), dst, recv).start()

    def to_owners(src, dst, send, recv, act):
        for u in range(2):
            ux = c if u == 0 else 3 - c
            for core in range(2):
                dev = ux * 4 + y * 2 + core

                @pl.when(dev != s)
                def _():
                    copy = remote(src.at[u, core], dst, send.at[u, core], recv, (dev, t))
                    copy.start() if act == "start" else copy.wait_send()

                if act == "start":

                    @pl.when(dev == s)
                    def _():
                        pltpu.make_async_copy(src.at[u, core], dst, recv).start()

    def q_moves(act):
        for a, ref in ((1, q_ref), (0, qd_ref)):
            to_heads(
                lambda hx, ref=ref: ref.at[:, lanes(hx, HD)],
                qq.at[unit, c, :, a * HD : (a + 1) * HD],
                q_send,
                q_recv,
                a,
                act,
            )

    kv_along_x(0)
    for a in range(4):
        kv_own(a)
    q_moves("start")
    pending.append(lambda: q_moves("wait"))
    owed["q"] = lambda: wait_for(qq, q_recv)
    for a in (1, 2, 3):
        kv_along_x(a)

    ends = []
    total = 0
    for f in range(FRAMES):
        total = total + frame_ref[f]
        ends.append(total)
    times = [time_ref[f] for f in range(FRAMES)]

    def frame_facts(pos):
        kend = jnp.zeros(pos.shape, jnp.int32) + ends[FRAMES - 1]
        level = jnp.zeros(pos.shape, jnp.int32) + times[FRAMES - 1]
        for f in range(FRAMES - 2, -1, -1):
            inside = pos < ends[f]
            kend = jnp.where(inside, ends[f], kend)
            level = jnp.where(inside, times[f], level)
        angle = (level.astype(F32) + 0.5) * (math.pi / (2 * TSTEPS))
        return kend, jnp.cos(angle), jnp.sin(angle)

    lane = lax.broadcasted_iota(jnp.int32, (1, NQ), 1)
    chip0 = 2 * c + y
    chip1 = 2 * (3 - c) + y
    qpos = jnp.where(lane < UNIT, UNIT * chip0 + lane, UNIT * chip1 + lane - UNIT)
    kend, cosq, sinq = frame_facts(qpos)

    rpos = s * ROWS + t * 20 + lax.broadcasted_iota(jnp.int32, (20, 1), 0)
    _, cosr, sinr = frame_facts(rpos)
    negb[...] = jnp.zeros_like(negb)
    negb[0:20, :] = sinr * cosr * noisy_ref[...].astype(F32) - cosr * cosr * vel_ref[...].astype(F32)

    n0 = chip0 + 2
    n1 = jnp.minimum(chip1 + 2, 8)

    def over_keys(body, carry):
        carry = lax.fori_loop(0, n0, lambda i, st: body(i, st, 0), carry)
        return lax.fori_loop(n0, n1, lambda i, st: body(i, st, 256), carry)

    def put(row, lo, part_row):
        if lo == 0:
            return part_row
        return jnp.concatenate([row[:, :lo], part_row], axis=1)

    kv_across(0)
    kv_across(1)
    kv_received(0)
    kv_across(2)
    due("q")
    kv_complete(0)

    def chunk(buf, i):
        return buf[i // 2, i % 2].reshape(UNIT, buf.shape[-1])

    def pass1(i, top, lo):
        keys = kk[i // 2, i % 2, :, :, :HD].reshape(UNIT, HD)
        queries = qq[...].reshape(NQ, 2 * HD)[lo:, HD:]
        sc = dot_nt(keys, queries) * SCALE
        kpos = i * UNIT + lax.broadcasted_iota(jnp.int32, (UNIT, 1), 0)
        sc = jnp.where(kpos < kend[:, lo:], sc, -1e30)
        sbuf[i, :, lo:] = sc
        return put(top, lo, jnp.maximum(top[:, lo:], jnp.max(sc, axis=0, keepdims=True)))

    top = over_keys(pass1, jnp.full((1, NQ), -1e30, F32))

    kv_across(3)
    kv_received(1)
    kv_complete(1)
    kv_received(2)

    def pass2(i, state, lo):
        den, tan = state
        st = dot_nt(chunk(kk, i), qq[...].reshape(NQ, 2 * HD)[lo:]) * SCALE
        p = jnp.exp(sbuf[i, :, lo:] - top[:, lo:])
        sbuf[i, :, lo:] = p
        stbuf[i, :, lo:] = st
        den = put(den, lo, den[:, lo:] + jnp.sum(p, axis=0, keepdims=True))
        tan = put(tan, lo, tan[:, lo:] + jnp.sum(p * st, axis=0, keepdims=True))
        return den, tan

    row0 = jnp.zeros((1, NQ), F32)
    den, tan = over_keys(pass2, (row0, row0))
    inv = 1.0 / den
    mean = tan * inv
    kv_received(3)
    kv_complete(2)
    kv_complete(3)

    acc1[...] = jnp.zeros_like(acc1)
    acc2[...] = jnp.zeros_like(acc2)

    def pass3(i, state, lo):
        p = sbuf[i, :, lo:] * inv[:, lo:]
        ph = p.astype(BF16)
        p16[i, :, lo:] = ph
        ds = (p * (stbuf[i, :, lo:] - mean[:, lo:])).astype(BF16)
        vals = chunk(vv, i)
        acc1[:, lo:] += dot_tn(vals, ph)
        acc2[:, lo:] += dot_tn(vals[:, :HD], ds)
        return state

    over_keys(pass3, 0)
    attn_t = acc1[0:HD, :].astype(BF16)
    tan_t = (acc2[...] + acc1[HD:, :]).astype(BF16)
    at_own[...] = attn_t
    u_t = (0.5 * cosq) * (cosq * attn_t.astype(F32) + sinq * tan_t.astype(F32))
    ublk[...] = u_t.T.astype(BF16).reshape(2, 2, ROWS, HD)
    to_owners(ublk, uown.at[:, lanes(head, HD)], u_send, u_recv, "start")
    owed["u"] = lambda: wait_for(uown, u_recv)
    pending.append(lambda: to_owners(ublk, uown.at[:, lanes(head, HD)], u_send, u_recv, "wait"))

    def at_view(py, hx):
        return at.at[py, c, lanes(hx, HD), :]

    pltpu.make_async_copy(at_own, at_view(y, x), atx_recv).start()
    launch(remote(at_own, at_view(y, x), aty_send, aty_recv, seq_dev(x, 1 - y, c)))
    owed["aty"] = lambda: wait_for(at_view(1 - y, x), aty_recv)
    for dx in far:
        launch(remote(at_own, at_view(y, x), atx_send.at[0, dx], atx_recv, seq_dev(ring(x, dx), y, c)))
    owed["atx"] = lambda: wait_for(at.at[y, c], atx_recv)

    def at_pass_on():
        due("aty")
        for dx in far:
            view = at_view(1 - y, x)
            launch(remote(view, view, atx_send.at[1, dx], at2_recv, seq_dev(ring(x, dx), y, c)))
        owed["at2"] = lambda: wait_for(at.at[1 - y, c, 0 : 3 * HD], at2_recv)

    due("w")
    due("u")
    u = uown[...]
    pick = (
        lax.broadcasted_iota(jnp.int32, (ROWS, 32), 0)
        == t * 20 + lax.broadcasted_iota(jnp.int32, (ROWS, 32), 1)
    ) & (lax.broadcasted_iota(jnp.int32, (ROWS, 32), 1) < 20)
    pick = pick.astype(F32).astype(BF16)

    def partial(pyh, pz, half):
        cols = pl.ds(pl.multiple_of((pyh * 4 + pz) * 512 + half * 256, 256), 256)
        return dot_nn(u, w[:, cols]) + dot_nn(pick, negb[:, cols].astype(BF16))

    for dz in range(4):
        part_b[dz] = partial(1 - yh, ring(z, dz), 1).astype(BF16)
    launch(remote(part_b, rx_b, rsb_send, rsb_recv, tp_dev(1 - yh, z)))
    owed["rsb"] = lambda: wait_for(rx_b, rsb_recv)

    for dz in far:
        for e in range(2):
            part_a[dz, e] = partial(yh if e == 0 else 1 - yh, ring(z, dz), 0).astype(BF16)
        copy = remote(part_a.at[dz], rx_a.at[dz], rsa_send.at[dz], rsa_recv.at[dz], tp_dev(yh, ring(z, dz)))
        launch(copy)
        owed["rsa", dz] = copy.wait_recv

    for dz in range(4):
        sum_b[dz] = partial(yh, ring(z, dz), 1)
    for e in range(2):
        sum_a[e] = partial(yh if e == 0 else 1 - yh, z, 0)

    at_pass_on()

    due("rsb")
    for dz in far:
        part_b2[dz] = (sum_b[dz] + rx_b[dz].astype(F32)).astype(BF16)
        copy = remote(part_b2.at[dz], rx_b2.at[dz], rsb2_send.at[dz], rsb2_recv.at[dz], tp_dev(yh, ring(z, dz)))
        launch(copy)
        owed["rsb2", dz] = copy.wait_recv
    for dz in far:
        due(("rsa", dz))
    other = sum_a[1]
    for dz in far:
        other = other + rx_a[dz, 1].astype(F32)
    part_a2[...] = other.astype(BF16)
    copy = remote(part_a2, rx_a2, rsa2_send, rsa2_recv, tp_dev(1 - yh, z))
    launch(copy)
    owed["rsa2"] = copy.wait_recv

    def cot_copy(a, src, dst, dev):
        sem = (a,) + dst
        copy = remote(cot.at[(a,) + src], cot.at[(a,) + dst], t_send.at[sem], t_recv.at[sem], dev)
        launch(copy)
        owed[("t",) + sem] = copy.wait_recv

    cot_b = sum_b[0] + rx_b[0].astype(F32)
    for dz in far:
        due(("rsb2", dz))
        cot_b = cot_b + rx_b2[dz].astype(F32)
    cot[1, 0, 0] = cot_b.astype(BF16)
    cot_copy(1, (0, 0), (1, 0), tp_dev(1 - yh, z))
    for dz in far:
        cot_copy(1, (0, 0), (0, dz), tp_dev(yh, ring(z, dz)))

    cot_a = sum_a[0]
    for dz in far:
        cot_a = cot_a + rx_a[dz, 0].astype(F32)
    due("rsa2")
    cot_a = cot_a + rx_a2[...].astype(F32)
    cot[0, 0, 0] = cot_a.astype(BF16)
    cot_copy(0, (0, 0), (1, 0), tp_dev(1 - yh, z))
    for dz in far:
        cot_copy(0, (0, 0), (0, dz), tp_dev(yh, ring(z, dz)))

    def sq_copy(buf, d, send, recv, dev, name):
        copy = remote(buf.at[0], buf.at[d], send.at[d], recv.at[d], dev)
        launch(copy)
        owed[name, d] = copy.wait_recv

    sq = jnp.sum(cot_a * cot_a + cot_b * cot_b, axis=0, keepdims=True)
    sq_tp[0] = jnp.zeros((8, 128), F32) + jnp.sum(sq, axis=1, keepdims=True)
    for d in range(1, 8):
        sq_copy(sq_tp, d, sqt_send, sqt_recv, (s, lax.rem(t + d, 8)), "sqt")

    def grad_part(a, dyh, dz):
        pyh = lax.rem(yh + dyh, 2)
        pz = lax.rem(z + 4 - dz, 4)
        cols = pl.ds(pl.multiple_of((pyh * 4 + pz) * 512 + a * 256, 256), 256)
        return dot_nt(cot[a, dyh, dz], w[:, cols])

    grad = grad_part(0, 0, 0) + grad_part(1, 0, 0)
    due(("t", 1, 1, 0))
    for dz in far:
        cot_copy(1, (1, 0), (1, dz), tp_dev(yh, ring(z, dz)))
    grad = grad + grad_part(1, 1, 0)
    for dz in (1, 3, 2):
        due(("t", 0, 0, dz))
        cot_copy(0, (0, dz), (1, dz), tp_dev(1 - yh, z))
    for dz in (1, 3, 2):
        grad = grad + grad_part(0, 0, dz)
        due(("t", 1, 0, dz))
        grad = grad + grad_part(1, 0, dz)
    for a, dz in ((0, 0), (0, 1), (0, 3), (0, 2), (1, 1), (1, 3), (1, 2)):
        due(("t", a, 1, dz))
        grad = grad + grad_part(a, 1, dz)
    g_tx[...] = grad.astype(BF16)

    def g_moves(act):
        to_heads(lambda hx: g_tx.at[:, lanes(hx, HD)], g.at[unit, c], g_send, g_recv, 0, act)

    g_moves("start")
    owed["g"] = lambda: wait_for(g, g_recv)
    pending.append(lambda: g_moves("wait"))

    row_half = pl.ds(pl.multiple_of(80 * (z % 2), 16), 80)
    chip_slot = y * 4 + home * 2 + unit

    def tw_send_all(act):
        for d in (8, 9, 7, 6, 10, 4, 12, 5, 11, 3, 13, 2, 14, 1, 15, 0):
            dest = lax.rem(s + d, 16)
            tt = dest // 2
            dyh = lax.rem(yh + tt // 4, 2)
            dz = lax.rem(z + 4 - tt % 4, 4)
            src = cot.at[dest % 2, dyh, dz, row_half, lanes(yh, HD)]
            dst = tw_part.at[chip_slot]
            if d:
                copy = remote(src, dst, tw_send.at[d], tw_recv, (dest, t))
                copy.start() if act == "start" else copy.wait_send()
            elif act == "start":
                pltpu.make_async_copy(src, dst, tw_recv).start()

    def tw_turn(act):
        @pl.when(c == z // 2)
        def _():
            tw_send_all(act)

    tw_turn("start")
    owed["tw"] = lambda: wait_for(tw_part, tw_recv)
    pending.append(lambda: tw_turn("wait"))

    sqv = sq_tp[0]
    for d in range(1, 8):
        due(("sqt", d))
        sqv = sqv + sq_tp[d]
    sq_seq[0] = sqv
    for d in range(1, 16):
        sq_copy(sq_seq, d, sqs_send, sqs_recv, (lax.rem(s + d, 16), t), "sqs")

    due("tw")
    tw_view = tw.at[:, z // 2, row_half, lanes(yh, HD)]
    pltpu.make_async_copy(tw_part, tw_view, twg_recv).start()
    for d in range(1, 8):
        launch(remote(tw_part, tw_view, twg_send.at[d], twg_recv, (s, lax.rem(t + d, 8))))
    owed["twg"] = lambda: wait_for(tw, twg_recv)

    due("g")
    gt = g[...].reshape(NQ, HD).astype(F32).T
    dterm = jnp.sum(gt * at_own[...].astype(F32), axis=0, keepdims=True)
    dqt[...] = jnp.zeros_like(dqt)

    def zero(i, state):
        dkv[:, i] = jnp.zeros((2, 2, ROWS, HD), BF16)
        return state

    lax.fori_loop(n1, 8, zero, 0)

    def back(i, state, lo):
        gq = g[...].reshape(NQ, HD)[lo:]
        queries = qq[...].reshape(NQ, 2 * HD)[lo:, HD:]
        keys = chunk(kk, i)[:, :HD]
        vals = chunk(vv, i)[:, :HD]
        ph = p16[i, :, lo:]
        dp = dot_nt(vals, gq)
        ds = (ph.astype(F32) * (dp - dterm[:, lo:])).astype(BF16)
        dkv[1, i] = dot_nn(ph, gq).astype(BF16).reshape(2, ROWS, HD)
        dkv[0, i] = (dot_nn(ds, queries) * SCALE).astype(BF16).reshape(2, ROWS, HD)
        dqt[:, lo:] += dot_tn(keys, ds)
        return state

    over_keys(back, 0)

    sib = remote(dkv.at[:, :, 1 - c], sib_rx, sib_send, sib_recv, (sibling, t))
    launch(sib)
    owed["sib"] = sib.wait_recv
    dq_tx[...] = (dqt[...] * SCALE).T.astype(BF16).reshape(2, 2, ROWS, HD)
    to_owners(dq_tx, dq_rx.at[:, lanes(head, HD)], dq_send, dq_recv, "start")
    owed["dq"] = lambda: wait_for(dq_rx, dq_recv)
    pending.append(lambda: to_owners(dq_tx, dq_rx.at[:, lanes(head, HD)], dq_send, dq_recv, "wait"))
    due("sib")
    dkv_tx[...] = (dkv[:, :, c].astype(F32) + sib_rx[...].astype(F32)).astype(BF16)

    def dkv_copy(dx, dy):
        cx = ring(x, dx)
        cy = lax.rem(y + dy, 2)
        slot = dx * 2 + dy
        return remote(
            dkv_tx.at[:, cx * 2 + cy],
            dkv_rx.at[slot],
            dkv_send.at[slot],
            dkv_recv.at[slot],
            seq_dev(cx, cy, c),
        )

    far_chips = [(dx, dy) for dx in (2, 1, 3, 0) for dy in (1, 0) if dx or dy]
    for dx, dy in far_chips:
        launch(dkv_copy(dx, dy))
        owed["dkv", dx, dy] = dkv_copy(dx, dy).wait_recv

    due("atx")
    due("at2")
    atf = remote(at.at[:, c], at.at[:, c], atf_send, atf_recv, (sibling, t))
    launch(atf)
    owed["atf"] = atf.wait_recv
    due("twg")
    due("atf")

    gw = jnp.zeros((512, 256), F32)
    for a in range(4):
        rows = tw[2 * a : 2 * a + 2].reshape(NQ, 256)
        gw = gw + dot_nn(at[a // 2, a % 2], rows)
    gw_out[...] = gw

    sqv = sq_seq[0]
    for d in range(1, 16):
        due(("sqs", d))
        sqv = sqv + sq_seq[d]
    ms_out[...] = sqv

    due("dq")
    dq_out[...] = dq_rx[...]

    for dx in range(4):
        hx = lax.rem(x + 4 - dx, 4)
        tot = [None, None]
        for dy in (0, 1):
            if dx or dy:
                due(("dkv", dx, dy))
            for a in range(2):
                piece = dkv_rx[dx * 2 + dy, a] if dx or dy else dkv_tx[a, m]
                piece = piece.astype(F32)
                tot[a] = piece if tot[a] is None else tot[a] + piece
        dk_out[:, lanes(hx, HD)] = tot[0]
        dv_out[:, lanes(hx, HD)] = tot[1]

    finish()


def scaled(ms_ref, *refs):
    scale = lax.rsqrt(ms_ref[0:1, 0:1] / (2560 * 4096) + 1e-05)
    for src, dst in zip(refs[:4], refs[4:]):
        dst[...] = (src[...].astype(F32) * scale).astype(BF16)


def on_device(q, k, v, qd, kd, vd, w, noisy, vel, time_index, frame_lengths):
    smem = pl.BlockSpec(memory_space=pltpu.SMEM)
    vmem = pl.BlockSpec(memory_space=pltpu.VMEM)
    hbm = pl.BlockSpec(memory_space=pl.ANY)
    dma = pltpu.SemaphoreType.DMA
    scratch = [
        pltpu.VMEM((512, 4096), BF16),
        pltpu.VMEM((4, 2, 2, ROWS, 256), BF16),
        pltpu.VMEM((4, 2, 2, ROWS, 256), BF16),
        pltpu.VMEM((2, 2, ROWS, 256), BF16),
        pltpu.VMEM((8, UNIT, NQ), F32),
        pltpu.VMEM((8, UNIT, NQ), F32),
        pltpu.VMEM((8, UNIT, NQ), BF16),
        pltpu.VMEM((256, NQ), F32),
        pltpu.VMEM((HD, NQ), F32),
        pltpu.VMEM((2, 2, ROWS, HD), BF16),
        pltpu.VMEM((ROWS, 512), BF16),
        pltpu.VMEM((HD, NQ), BF16),
        pltpu.VMEM((2, 2, 512, NQ), BF16),
        pltpu.VMEM((32, 4096), F32),
        pltpu.VMEM((4, 2, ROWS, 256), BF16),
        pltpu.VMEM((4, ROWS, 256), BF16),
        pltpu.VMEM((4, 2, ROWS, 256), BF16),
        pltpu.VMEM((4, ROWS, 256), BF16),
        pltpu.VMEM((2, ROWS, 256), F32),
        pltpu.VMEM((4, ROWS, 256), F32),
        pltpu.VMEM((ROWS, 256), BF16),
        pltpu.VMEM((4, ROWS, 256), BF16),
        pltpu.VMEM((ROWS, 256), BF16),
        pltpu.VMEM((4, ROWS, 256), BF16),
        pltpu.VMEM((2, 2, 4, ROWS, 256), BF16),
        pltpu.VMEM((ROWS, 512), BF16),
        pltpu.VMEM((2, 2, ROWS, HD), BF16),
        pltpu.VMEM((HD, NQ), F32),
        pltpu.VMEM((2, 2, ROWS, HD), BF16),
        pltpu.VMEM((ROWS, 512), BF16),
        pltpu.VMEM((2, 8, 2, ROWS, HD), BF16),
        pltpu.VMEM((2, 8, ROWS, HD), BF16),
        pltpu.VMEM((2, 8, ROWS, HD), BF16),
        pltpu.VMEM((8, 2, ROWS, HD), BF16),
        pltpu.VMEM((8, 80, HD), BF16),
        pltpu.VMEM((8, 2, ROWS, 256), BF16),
        pltpu.VMEM((8, 8, 128), F32),
        pltpu.VMEM((16, 8, 128), F32),
        dma,
        dma((4, 4)),
        dma((4,)),
        dma((4, 4)),
        dma((4,)),
        dma((4,)),
        dma((4,)),
        dma((4,)),
        dma((4,)),
        dma((2, 4)),
        dma,
        dma((2, 2)),
        dma,
        dma((2, 4)),
        dma,
        dma,
        dma,
        dma,
        dma,
        dma,
        dma((4,)),
        dma((4,)),
        dma,
        dma,
        dma,
        dma,
        dma((4,)),
        dma((4,)),
        dma((2, 2, 4)),
        dma((2, 2, 4)),
        dma((1, 4)),
        dma,
        dma((16,)),
        dma,
        dma((8,)),
        dma,
        dma((2, 2)),
        dma,
        dma,
        dma,
        dma((8,)),
        dma((8,)),
        dma((8,)),
        dma((8,)),
        dma((16,)),
        dma((16,)),
    ]
    dq, dk, dv, gw, ms = pl.pallas_call(
        kernel,
        out_shape=(
            jax.ShapeDtypeStruct((ROWS, 512), BF16),
            jax.ShapeDtypeStruct((ROWS, 512), F32),
            jax.ShapeDtypeStruct((ROWS, 512), F32),
            jax.ShapeDtypeStruct((512, 256), F32),
            jax.ShapeDtypeStruct((8, 128), F32),
        ),
        in_specs=[smem, smem] + [hbm] * 7 + [vmem] * 2,
        out_specs=(vmem,) * 5,
        scratch_shapes=scratch,
        compiler_params=pltpu.CompilerParams(
            collective_id=0, has_side_effects=True, vmem_limit_bytes=56 * 1024 * 1024
        ),
        cost_estimate=pl.CostEstimate(flops=7 * 10**9, bytes_accessed=8 * 10**6, transcendentals=1638400),
    )(frame_lengths, time_index, q, k, v, qd, kd, vd, w, noisy, vel)
    return pl.pallas_call(
        scaled,
        out_shape=tuple(jax.ShapeDtypeStruct(part.shape, BF16) for part in (dq, dk, dv, gw)),
        in_specs=[vmem] * 5,
        out_specs=(vmem,) * 4,
    )(ms, dq, dk, dv, gw)


def solution(mesh):
    in_specs = (P("seq", "tp"),) * 6 + (P("tp", None), P(("seq", "tp"), None), P(("seq", "tp"), None), P(), P())
    out_specs = (P("seq", "tp"), P("seq", "tp"), P("seq", "tp"), P("tp", "seq"))
    return jax.shard_map(
        on_device, mesh=mesh, in_specs=in_specs, out_specs=out_specs, check_vma=False
    )
```

time: 128 us -> 110 us (0.86)
  the two profiles are of different devices: /device:TPU:1 before, /device:TPU:17 now
where the time goes in v2:
time: 110 us
  Pallas kernels  109 us (99%)
    pallas_call x1, Pallas kernels, on_device(): pl.pallas_call(kernel, out_shape=(jax.ShapeDtypeStruct((ROWS, 512), BF16)...  107 us
    pallas_call x1, Pallas kernels, on_device(): pl.pallas_call(scaled, out_shape=tuple((jax.ShapeDtypeStruct(part.shape,...  2.27 us

profile of v2, /device:TPU:17, one launch (start us, length us, event | category | flops | bytes accessed | tf_op | source)
XLA Modules:
  0.0 109.7 jit_solution(15919760494828716242)
XLA Ops:
  0.6 106.8 %shard_map.138 = (bf16[160,512]{1,0:T(8,128)(2,1)}, f32[160,512]{1,0:T(8,128)}, f32[160,512]{1,0:T(8,128)}, f32[512,256]{1,0:T(8,128)}, f32[8,128]{1,0:T(8,128)}) custom-call(s32[16]{0:T(128)} %frame_ref.1, s32[16]{0:T(128)} %time_ref.1, bf16[160,512]{1,0:T(8,128)(2,1)} %q_ref.1, bf16[160,512]{1,0:T(8,128)(2,1)} %k_ref.1, bf16[160,512]{1,0:T(8,128)(2,1)} %v_ref.1, ...), custom_call_target="tpu_custom_call" | custom-call | flops 7000000000 | bytes 8000000 | tf_op jit(solution)/shard_map/pallas_call | solution.py:775
  107.5 2.3 %shard_map.139 = (bf16[160,512]{1,0:T(8,128)(2,1)}, bf16[160,512]{1,0:T(8,128)(2,1)}, bf16[160,512]{1,0:T(8,128)(2,1)}, bf16[512,256]{1,0:T(8,128)(2,1)}) custom-call(f32[8,128]{1,0:T(8,128)} %get-tuple-element.9.ms_ref, bf16[160,512]{1,0:T(8,128)(2,1)} %get-tuple-element.10.refs_0_, f32[160,512]{1,0:T(8,128)} %get-tuple-element.11.refs_1_, ...), custom_call_target="tpu_custom_call" | custom-call | tf_op jit(solution)/shard_map/pallas_call | solution.py:792

commit v3 on v2

--- a/solution.py
+++ b/solution.py
@@ -154,6 +154,9 @@
     def tp_dev(pyh, pz):
         return (s, pyh * 4 + pz)
 
+    def local_copy(src, dst, sem):
+        return pltpu.make_async_copy(src, dst, sem)
+
     def remote(src, dst, ssem, rsem, dev):
         return pltpu.make_async_remote_copy(
             src_ref=src, dst_ref=dst, send_sem=ssem, recv_sem=rsem, device_id=dev, device_id_type=MESH
@@ -188,11 +191,12 @@
 
     barrier = pltpu.get_barrier_semaphore()
     sibling = s + 1 - 2 * c
-    for d in range(1, 16):
-        pl.semaphore_signal(barrier, inc=1, device_id=(lax.rem(s + d, 16), t), device_id_type=MESH)
-    for d in range(1, 8):
-        pl.semaphore_signal(barrier, inc=1, device_id=(s, lax.rem(t + d, 8)), device_id_type=MESH)
-    pl.semaphore_wait(barrier, 22)
+    partners = [seq_dev(x, 1 - y, c), (sibling, t), tp_dev(1 - yh, z)]
+    for dx in far:
+        partners += [seq_dev(ring(x, dx), y, c), seq_dev(ring(x, dx), y, 1 - c), tp_dev(yh, ring(z, dx))]
+    for dev in partners:
+        pl.semaphore_signal(barrier, inc=1, device_id=dev, device_id_type=MESH)
+    pl.semaphore_wait(barrier, len(partners))
 
     kv_src = (k_ref, kd_ref, v_ref, vd_ref)
     kv_dst = ((kk, 0), (kk, 1), (vv, 0), (vv, 1))
@@ -208,7 +212,7 @@
         return kv_view(a, slice(None), py, pc)
 
     def kv_own(a):
-        pltpu.make_async_copy(kv_piece(a, x), kv_view(a, x, y, c), kvx_recv.at[a]).start()
+        local_copy(kv_piece(a, x), kv_view(a, x, y, c), kvx_recv.at[a]).start()
         launch(
             remote(
                 kv_piece(a, x), kv_view(a, x, y, c), kvy_send.at[a, 0], kvy_recv.at[a], seq_dev(x, 1 - y, c)
@@ -266,7 +270,7 @@
 
                     @pl.when(home == c)
                     def _():
-                        pltpu.make_async_copy(src_of(hx), dst, recv).start()
+                        local_copy(src_of(hx), dst, recv).start()
 
     def to_owners(src, dst, send, recv, act):
         for u in range(2):
@@ -283,7 +287,7 @@
 
                     @pl.when(dev == s)
                     def _():
-                        pltpu.make_async_copy(src.at[u, core], dst, recv).start()
+                        local_copy(src.at[u, core], dst, recv).start()
 
     def q_moves(act):
         for a, ref in ((1, q_ref), (0, qd_ref)):
@@ -369,7 +373,6 @@
     kv_across(3)
     kv_received(1)
     kv_complete(1)
-    kv_received(2)
 
     def pass2(i, state, lo):
         den, tan = state
@@ -385,9 +388,9 @@
     den, tan = over_keys(pass2, (row0, row0))
     inv = 1.0 / den
     mean = tan * inv
+    kv_received(2)
     kv_received(3)
     kv_complete(2)
-    kv_complete(3)
 
     acc1[...] = jnp.zeros_like(acc1)
     acc2[...] = jnp.zeros_like(acc2)
@@ -397,14 +400,22 @@
         ph = p.astype(BF16)
         p16[i, :, lo:] = ph
         ds = (p * (stbuf[i, :, lo:] - mean[:, lo:])).astype(BF16)
-        vals = chunk(vv, i)
+        vals = vv[i // 2, i % 2, :, :, :HD].reshape(UNIT, HD)
         acc1[:, lo:] += dot_tn(vals, ph)
-        acc2[:, lo:] += dot_tn(vals[:, :HD], ds)
+        acc2[:, lo:] += dot_tn(vals, ds)
         return state
 
     over_keys(pass3, 0)
-    attn_t = acc1[0:HD, :].astype(BF16)
-    tan_t = (acc2[...] + acc1[HD:, :]).astype(BF16)
+    kv_complete(3)
+
+    def pass4(i, state, lo):
+        vals_dot = vv[i // 2, i % 2, :, :, HD:].reshape(UNIT, HD)
+        acc2[:, lo:] += dot_tn(vals_dot, p16[i, :, lo:])
+        return state
+
+    over_keys(pass4, 0)
+    attn_t = acc1[...].astype(BF16)
+    tan_t = acc2[...].astype(BF16)
     at_own[...] = attn_t
     u_t = (0.5 * cosq) * (cosq * attn_t.astype(F32) + sinq * tan_t.astype(F32))
     ublk[...] = u_t.T.astype(BF16).reshape(2, 2, ROWS, HD)
@@ -415,7 +426,7 @@
     def at_view(py, hx):
         return at.at[py, c, lanes(hx, HD), :]
 
-    pltpu.make_async_copy(at_own, at_view(y, x), atx_recv).start()
+    local_copy(at_own, at_view(y, x), atx_recv).start()
     launch(remote(at_own, at_view(y, x), aty_send, aty_recv, seq_dev(x, 1 - y, c)))
     owed["aty"] = lambda: wait_for(at_view(1 - y, x), aty_recv)
     for dx in far:
@@ -557,7 +568,7 @@
                 copy = remote(src, dst, tw_send.at[d], tw_recv, (dest, t))
                 copy.start() if act == "start" else copy.wait_send()
             elif act == "start":
-                pltpu.make_async_copy(src, dst, tw_recv).start()
+                local_copy(src, dst, tw_recv).start()
 
     def tw_turn(act):
         @pl.when(c == z // 2)
@@ -577,24 +588,43 @@
         sq_copy(sq_seq, d, sqs_send, sqs_recv, (lax.rem(s + d, 16), t), "sqs")
 
     due("tw")
-    tw_view = tw.at[:, z // 2, row_half, lanes(yh, HD)]
-    pltpu.make_async_copy(tw_part, tw_view, twg_recv).start()
-    for d in range(1, 8):
-        launch(remote(tw_part, tw_view, twg_send.at[d], twg_recv, (s, lax.rem(t + d, 8))))
-    owed["twg"] = lambda: wait_for(tw, twg_recv)
+
+    def tw_view(a, dyh, dz):
+        pyh = lax.rem(yh + dyh, 2)
+        pz = lax.rem(z + 4 - dz, 4)
+        rows = pl.ds(pl.multiple_of(80 * (pz % 2), 16), 80)
+        return tw.at[4 * a : 4 * a + 4, pz // 2, rows, lanes(pyh, HD)]
+
+    def twg_copy(a, origin, slot, dev):
+        view = tw_view(a, *origin)
+        src = tw_part.at[4 * a : 4 * a + 4] if origin == (0, 0) else view
+        sem = (a,) + slot
+        copy = remote(src, view, twg_send.at[sem], twg_recv.at[sem], dev)
+        launch(copy)
+        owed[("twg",) + sem] = copy.wait_recv
+
+    for a in range(2):
+        local_copy(tw_part.at[4 * a : 4 * a + 4], tw_view(a, 0, 0), twg_recv.at[a, 0, 0]).start()
+        owed["twg", a, 0, 0] = lambda a=a: wait_for(tw_view(a, 0, 0), twg_recv.at[a, 0, 0])
+        for dz in far:
+            twg_copy(a, (0, 0), (0, dz), tp_dev(yh, ring(z, dz)))
+    for a in (1, 0):
+        twg_copy(a, (0, 0), (1, 0), tp_dev(1 - yh, z))
+
+    def tw_pass_on():
+        due(("twg", 1, 1, 0))
+        for dz in far:
+            twg_copy(1, (1, 0), (1, dz), tp_dev(yh, ring(z, dz)))
+        for dz in (1, 3, 2):
+            due(("twg", 0, 0, dz))
+            twg_copy(0, (0, dz), (1, dz), tp_dev(1 - yh, z))
 
     due("g")
     gt = g[...].reshape(NQ, HD).astype(F32).T
     dterm = jnp.sum(gt * at_own[...].astype(F32), axis=0, keepdims=True)
     dqt[...] = jnp.zeros_like(dqt)
 
-    def zero(i, state):
-        dkv[:, i] = jnp.zeros((2, 2, ROWS, HD), BF16)
-        return state
-
-    lax.fori_loop(n1, 8, zero, 0)
-
-    def back(i, state, lo):
+    def back(i, lo):
         gq = g[...].reshape(NQ, HD)[lo:]
         queries = qq[...].reshape(NQ, 2 * HD)[lo:, HD:]
         keys = chunk(kk, i)[:, :HD]
@@ -605,43 +635,64 @@
         dkv[1, i] = dot_nn(ph, gq).astype(BF16).reshape(2, ROWS, HD)
         dkv[0, i] = (dot_nn(ds, queries) * SCALE).astype(BF16).reshape(2, ROWS, HD)
         dqt[:, lo:] += dot_tn(keys, ds)
+
+    def sib_copy(i):
+        return remote(
+            dkv.at[:, i, 1 - c], sib_rx.at[:, i], sib_send.at[i], sib_recv.at[i], (sibling, t)
+        )
+
+    def dkv_copy(i):
+        return remote(
+            dkv_tx.at[:, i], dkv_rx.at[m], dkv_send.at[i], dkv_recv.at[m], seq_dev(i // 2, i % 2, c)
+        )
+
+    def both_cores(i):
+        sib_copy(i).wait_recv()
+        return dkv[:, i, c].astype(F32) + sib_rx[:, i].astype(F32)
+
+    def back_step(k, state):
+        i = lax.rem(m + 1 + k, 8)
+
+        @pl.when(i < n0)
+        def _():
+            back(i, 0)
+
+        @pl.when((i >= n0) & (i < n1))
+        def _():
+            back(i, 256)
+
+        @pl.when(i >= n1)
+        def _():
+            dkv[:, i] = jnp.zeros((2, 2, ROWS, HD), BF16)
+
+        sib_copy(i).start()
+
+        @pl.when(k > 0)
+        def _():
+            done = lax.rem(m + k, 8)
+            dkv_tx[:, done] = both_cores(done).astype(BF16)
+            dkv_copy(done).start()
+
         return state
 
-    over_keys(back, 0)
-
-    sib = remote(dkv.at[:, :, 1 - c], sib_rx, sib_send, sib_recv, (sibling, t))
-    launch(sib)
-    owed["sib"] = sib.wait_recv
+    lax.fori_loop(0, 8, back_step, 0)
     dq_tx[...] = (dqt[...] * SCALE).T.astype(BF16).reshape(2, 2, ROWS, HD)
     to_owners(dq_tx, dq_rx.at[:, lanes(head, HD)], dq_send, dq_recv, "start")
     owed["dq"] = lambda: wait_for(dq_rx, dq_recv)
     pending.append(lambda: to_owners(dq_tx, dq_rx.at[:, lanes(head, HD)], dq_send, dq_recv, "wait"))
-    due("sib")
-    dkv_tx[...] = (dkv[:, :, c].astype(F32) + sib_rx[...].astype(F32)).astype(BF16)
-
-    def dkv_copy(dx, dy):
-        cx = ring(x, dx)
-        cy = lax.rem(y + dy, 2)
-        slot = dx * 2 + dy
-        return remote(
-            dkv_tx.at[:, cx * 2 + cy],
-            dkv_rx.at[slot],
-            dkv_send.at[slot],
-            dkv_recv.at[slot],
-            seq_dev(cx, cy, c),
-        )
-
-    far_chips = [(dx, dy) for dx in (2, 1, 3, 0) for dy in (1, 0) if dx or dy]
-    for dx, dy in far_chips:
-        launch(dkv_copy(dx, dy))
-        owed["dkv", dx, dy] = dkv_copy(dx, dy).wait_recv
+    tw_pass_on()
+    dkv_rx[m] = both_cores(m).astype(BF16)
 
     due("atx")
     due("at2")
     atf = remote(at.at[:, c], at.at[:, c], atf_send, atf_recv, (sibling, t))
     launch(atf)
     owed["atf"] = atf.wait_recv
-    due("twg")
+    for a in range(2):
+        for dyh in range(2):
+            for dz in range(4):
+                if ("twg", a, dyh, dz) in owed:
+                    due(("twg", a, dyh, dz))
     due("atf")
 
     gw = jnp.zeros((512, 256), F32)
@@ -659,19 +710,21 @@
     due("dq")
     dq_out[...] = dq_rx[...]
 
-    for dx in range(4):
-        hx = lax.rem(x + 4 - dx, 4)
-        tot = [None, None]
-        for dy in (0, 1):
-            if dx or dy:
-                due(("dkv", dx, dy))
-            for a in range(2):
-                piece = dkv_rx[dx * 2 + dy, a] if dx or dy else dkv_tx[a, m]
-                piece = piece.astype(F32)
-                tot[a] = piece if tot[a] is None else tot[a] + piece
-        dk_out[:, lanes(hx, HD)] = tot[0]
-        dv_out[:, lanes(hx, HD)] = tot[1]
-
+    def all_dkv(k, state):
+        i = lax.rem(m + 1 + k, 8)
+        sib_copy(i).wait_send()
+
+        @pl.when(k < 7)
+        def _():
+            dkv_copy(i).wait_send()
+            remote(dkv_tx.at[:, i], dkv_rx.at[i], dkv_send.at[i], dkv_recv.at[i], (sibling, t)).wait_recv()
+
+        return state
+
+    lax.fori_loop(0, 8, all_dkv, 0)
+    for h in range(4):
+        for a, out in enumerate((dk_out, dv_out)):
+            out[:, h * HD : (h + 1) * HD] = dkv_rx[2 * h, a].astype(F32) + dkv_rx[2 * h + 1, a].astype(F32)
     finish()
 
 
@@ -694,7 +747,7 @@
         pltpu.VMEM((8, UNIT, NQ), F32),
         pltpu.VMEM((8, UNIT, NQ), F32),
         pltpu.VMEM((8, UNIT, NQ), BF16),
-        pltpu.VMEM((256, NQ), F32),
+        pltpu.VMEM((HD, NQ), F32),
         pltpu.VMEM((HD, NQ), F32),
         pltpu.VMEM((2, 2, ROWS, HD), BF16),
         pltpu.VMEM((ROWS, 512), BF16),
@@ -759,12 +812,12 @@
         dma,
         dma((16,)),
         dma,
+        dma((2, 2, 4)),
+        dma((2, 2, 4)),
+        dma((2, 2)),
+        dma,
         dma((8,)),
-        dma,
-        dma((2, 2)),
-        dma,
-        dma,
-        dma,
+        dma((8,)),
         dma((8,)),
         dma((8,)),
         dma((8,)),

time: 110 us -> 106 us (0.964)
  the two profiles are of different devices: /device:TPU:17 before, /device:TPU:1 now
where the time goes in v3:
time: 106 us
  Pallas kernels  105 us (99%)
    pallas_call x1, Pallas kernels, on_device(): pl.pallas_call(kernel, out_shape=(jax.ShapeDtypeStruct((ROWS, 512), BF16)...  103 us
    pallas_call x1, Pallas kernels, on_device(): pl.pallas_call(scaled, out_shape=tuple((jax.ShapeDtypeStruct(part.shape,...  2.27 us

profile of v3, /device:TPU:1, one launch (start us, length us, event | category | flops | bytes accessed | tf_op | source)
XLA Modules:
  0.0 105.7 jit_solution(7461887237449309925)
XLA Ops:
  0.6 102.8 %shard_map.138 = (bf16[160,512]{1,0:T(8,128)(2,1)}, f32[160,512]{1,0:T(8,128)}, f32[160,512]{1,0:T(8,128)}, f32[512,256]{1,0:T(8,128)}, f32[8,128]{1,0:T(8,128)}) custom-call(s32[16]{0:T(128)} %frame_ref.1, s32[16]{0:T(128)} %time_ref.1, bf16[160,512]{1,0:T(8,128)(2,1)} %q_ref.1, bf16[160,512]{1,0:T(8,128)(2,1)} %k_ref.1, bf16[160,512]{1,0:T(8,128)(2,1)} %v_ref.1, ...), custom_call_target="tpu_custom_call" | custom-call | flops 7000000000 | bytes 8000000 | tf_op jit(solution)/shard_map/pallas_call | solution.py:828
  103.5 2.3 %shard_map.139 = (bf16[160,512]{1,0:T(8,128)(2,1)}, bf16[160,512]{1,0:T(8,128)(2,1)}, bf16[160,512]{1,0:T(8,128)(2,1)}, bf16[512,256]{1,0:T(8,128)(2,1)}) custom-call(f32[8,128]{1,0:T(8,128)} %get-tuple-element.9.ms_ref, bf16[160,512]{1,0:T(8,128)(2,1)} %get-tuple-element.10.refs_0_, f32[160,512]{1,0:T(8,128)} %get-tuple-element.11.refs_1_, ...), custom_call_target="tpu_custom_call" | custom-call | tf_op jit(solution)/shard_map/pallas_call | solution.py:845

commit v4 on v3

--- a/solution.py
+++ b/solution.py
@@ -303,11 +303,12 @@
     kv_along_x(0)
     for a in range(4):
         kv_own(a)
+    kv_along_x(1)
+    kv_along_x(2)
     q_moves("start")
     pending.append(lambda: q_moves("wait"))
     owed["q"] = lambda: wait_for(qq, q_recv)
-    for a in (1, 2, 3):
-        kv_along_x(a)
+    kv_along_x(3)
 
     ends = []
     total = 0
@@ -340,8 +341,10 @@
     n0 = chip0 + 2
     n1 = jnp.minimum(chip1 + 2, 8)
 
-    def over_keys(body, carry):
+    def over_keys(body, carry, between=None):
         carry = lax.fori_loop(0, n0, lambda i, st: body(i, st, 0), carry)
+        if between is not None:
+            between()
         return lax.fori_loop(n0, n1, lambda i, st: body(i, st, 256), carry)
 
     def put(row, lo, part_row):
@@ -351,8 +354,9 @@
 
     kv_across(0)
     kv_across(1)
+    kv_across(2)
     kv_received(0)
-    kv_across(2)
+    kv_received(1)
     due("q")
     kv_complete(0)
 
@@ -371,7 +375,6 @@
     top = over_keys(pass1, jnp.full((1, NQ), -1e30, F32))
 
     kv_across(3)
-    kv_received(1)
     kv_complete(1)
 
     def pass2(i, state, lo):
@@ -385,11 +388,9 @@
         return den, tan
 
     row0 = jnp.zeros((1, NQ), F32)
-    den, tan = over_keys(pass2, (row0, row0))
+    den, tan = over_keys(pass2, (row0, row0), lambda: kv_received(2))
     inv = 1.0 / den
     mean = tan * inv
-    kv_received(2)
-    kv_received(3)
     kv_complete(2)
 
     acc1[...] = jnp.zeros_like(acc1)
@@ -405,7 +406,7 @@
         acc2[:, lo:] += dot_tn(vals, ds)
         return state
 
-    over_keys(pass3, 0)
+    over_keys(pass3, 0, lambda: kv_received(3))
     kv_complete(3)
 
     def pass4(i, state, lo):
@@ -426,13 +427,6 @@
     def at_view(py, hx):
         return at.at[py, c, lanes(hx, HD), :]
 
-    local_copy(at_own, at_view(y, x), atx_recv).start()
-    launch(remote(at_own, at_view(y, x), aty_send, aty_recv, seq_dev(x, 1 - y, c)))
-    owed["aty"] = lambda: wait_for(at_view(1 - y, x), aty_recv)
-    for dx in far:
-        launch(remote(at_own, at_view(y, x), atx_send.at[0, dx], atx_recv, seq_dev(ring(x, dx), y, c)))
-    owed["atx"] = lambda: wait_for(at.at[y, c], atx_recv)
-
     def at_pass_on():
         due("aty")
         for dx in far:
@@ -455,73 +449,97 @@
 
     for dz in range(4):
         part_b[dz] = partial(1 - yh, ring(z, dz), 1).astype(BF16)
-    launch(remote(part_b, rx_b, rsb_send, rsb_recv, tp_dev(1 - yh, z)))
-    owed["rsb"] = lambda: wait_for(rx_b, rsb_recv)
+    halves = [slice(0, 80), slice(80, 160)]
+
+    def stage(name, key, src, dst, send, recv, dev):
+        copy = remote(src, dst, send.at[key], recv.at[key], dev)
+        launch(copy)
+        owed[(name,) + key] = copy.wait_recv
+
+    def send_b(hf):
+        rows = halves[hf]
+        stage("rsb", (hf,), part_b.at[:, rows], rx_b.at[:, rows], rsb_send, rsb_recv, tp_dev(1 - yh, z))
+
+    send_b(0)
 
     for dz in far:
         for e in range(2):
             part_a[dz, e] = partial(yh if e == 0 else 1 - yh, ring(z, dz), 0).astype(BF16)
-        copy = remote(part_a.at[dz], rx_a.at[dz], rsa_send.at[dz], rsa_recv.at[dz], tp_dev(yh, ring(z, dz)))
-        launch(copy)
-        owed["rsa", dz] = copy.wait_recv
+
+    def send_a(hf):
+        rows = halves[hf]
+        for dz in far:
+            dev = tp_dev(yh, ring(z, dz))
+            stage("rsa", (hf, dz), part_a.at[dz, :, rows], rx_a.at[dz, :, rows], rsa_send, rsa_recv, dev)
+
+    send_a(0)
+    send_b(1)
+    send_a(1)
+
+    local_copy(at_own, at_view(y, x), atx_recv).start()
+    launch(remote(at_own, at_view(y, x), aty_send, aty_recv, seq_dev(x, 1 - y, c)))
+    owed["aty"] = lambda: wait_for(at_view(1 - y, x), aty_recv)
+    for dx in far:
+        launch(remote(at_own, at_view(y, x), atx_send.at[0, dx], atx_recv, seq_dev(ring(x, dx), y, c)))
+    owed["atx"] = lambda: wait_for(at.at[y, c], atx_recv)
 
     for dz in range(4):
         sum_b[dz] = partial(yh, ring(z, dz), 1)
     for e in range(2):
         sum_a[e] = partial(yh if e == 0 else 1 - yh, z, 0)
 
-    at_pass_on()
-
-    due("rsb")
-    for dz in far:
-        part_b2[dz] = (sum_b[dz] + rx_b[dz].astype(F32)).astype(BF16)
-        copy = remote(part_b2.at[dz], rx_b2.at[dz], rsb2_send.at[dz], rsb2_recv.at[dz], tp_dev(yh, ring(z, dz)))
-        launch(copy)
-        owed["rsb2", dz] = copy.wait_recv
-    for dz in far:
-        due(("rsa", dz))
-    other = sum_a[1]
-    for dz in far:
-        other = other + rx_a[dz, 1].astype(F32)
-    part_a2[...] = other.astype(BF16)
-    copy = remote(part_a2, rx_a2, rsa2_send, rsa2_recv, tp_dev(1 - yh, z))
-    launch(copy)
-    owed["rsa2"] = copy.wait_recv
-
-    def cot_copy(a, src, dst, dev):
-        sem = (a,) + dst
-        copy = remote(cot.at[(a,) + src], cot.at[(a,) + dst], t_send.at[sem], t_recv.at[sem], dev)
-        launch(copy)
-        owed[("t",) + sem] = copy.wait_recv
-
-    cot_b = sum_b[0] + rx_b[0].astype(F32)
-    for dz in far:
-        due(("rsb2", dz))
-        cot_b = cot_b + rx_b2[dz].astype(F32)
-    cot[1, 0, 0] = cot_b.astype(BF16)
-    cot_copy(1, (0, 0), (1, 0), tp_dev(1 - yh, z))
-    for dz in far:
-        cot_copy(1, (0, 0), (0, dz), tp_dev(yh, ring(z, dz)))
-
-    cot_a = sum_a[0]
-    for dz in far:
-        cot_a = cot_a + rx_a[dz, 0].astype(F32)
-    due("rsa2")
-    cot_a = cot_a + rx_a2[...].astype(F32)
-    cot[0, 0, 0] = cot_a.astype(BF16)
-    cot_copy(0, (0, 0), (1, 0), tp_dev(1 - yh, z))
-    for dz in far:
-        cot_copy(0, (0, 0), (0, dz), tp_dev(yh, ring(z, dz)))
+
+    def cot_copy(a, src, dst, dev, hf):
+        rows = halves[hf]
+        sem = (a,) + dst + (hf,)
+        stage("t", sem, cot.at[(a,) + src + (rows,)], cot.at[(a,) + dst + (rows,)], t_send, t_recv, dev)
+
+    for hf in range(2):
+        rows = halves[hf]
+        due(("rsb", hf))
+        for dz in far:
+            part_b2[dz, rows] = (sum_b[dz, rows] + rx_b[dz, rows].astype(F32)).astype(BF16)
+            dev = tp_dev(yh, ring(z, dz))
+            stage("rsb2", (hf, dz), part_b2.at[dz, rows], rx_b2.at[dz, rows], rsb2_send, rsb2_recv, dev)
+        other = sum_a[1, rows]
+        for dz in far:
+            due(("rsa", hf, dz))
+            other = other + rx_a[dz, 1, rows].astype(F32)
+        part_a2[rows] = other.astype(BF16)
+        stage("rsa2", (hf,), part_a2.at[rows], rx_a2.at[rows], rsa2_send, rsa2_recv, tp_dev(1 - yh, z))
+
+    sq = jnp.zeros((1, 256), F32)
+    for hf in range(2):
+        rows = halves[hf]
+        cot_a = sum_a[0, rows]
+        for dz in far:
+            cot_a = cot_a + rx_a[dz, 0, rows].astype(F32)
+        due(("rsa2", hf))
+        cot_a = cot_a + rx_a2[rows].astype(F32)
+        cot[0, 0, 0, rows] = cot_a.astype(BF16)
+        for dz in far:
+            cot_copy(0, (0, 0), (0, dz), tp_dev(yh, ring(z, dz)), hf)
+        cot_b = sum_b[0, rows] + rx_b[0, rows].astype(F32)
+        for dz in far:
+            due(("rsb2", hf, dz))
+            cot_b = cot_b + rx_b2[dz, rows].astype(F32)
+        cot[1, 0, 0, rows] = cot_b.astype(BF16)
+        cot_copy(1, (0, 0), (1, 0), tp_dev(1 - yh, z), hf)
+        for dz in far:
+            cot_copy(1, (0, 0), (0, dz), tp_dev(yh, ring(z, dz)), hf)
+        cot_copy(0, (0, 0), (1, 0), tp_dev(1 - yh, z), hf)
+        sq = sq + jnp.sum(cot_a * cot_a + cot_b * cot_b, axis=0, keepdims=True)
 
     def sq_copy(buf, d, send, recv, dev, name):
         copy = remote(buf.at[0], buf.at[d], send.at[d], recv.at[d], dev)
         launch(copy)
         owed[name, d] = copy.wait_recv
 
-    sq = jnp.sum(cot_a * cot_a + cot_b * cot_b, axis=0, keepdims=True)
     sq_tp[0] = jnp.zeros((8, 128), F32) + jnp.sum(sq, axis=1, keepdims=True)
     for d in range(1, 8):
         sq_copy(sq_tp, d, sqt_send, sqt_recv, (s, lax.rem(t + d, 8)), "sqt")
+
+    at_pass_on()
 
     def grad_part(a, dyh, dz):
         pyh = lax.rem(yh + dyh, 2)
@@ -530,19 +548,22 @@
         return dot_nt(cot[a, dyh, dz], w[:, cols])
 
     grad = grad_part(0, 0, 0) + grad_part(1, 0, 0)
-    due(("t", 1, 1, 0))
-    for dz in far:
-        cot_copy(1, (1, 0), (1, dz), tp_dev(yh, ring(z, dz)))
+    for hf in range(2):
+        due(("t", 1, 1, 0, hf))
+        for dz in far:
+            cot_copy(1, (1, 0), (1, dz), tp_dev(yh, ring(z, dz)), hf)
+        for dz in (1, 3, 2):
+            due(("t", 0, 0, dz, hf))
+            cot_copy(0, (0, dz), (1, dz), tp_dev(1 - yh, z), hf)
     grad = grad + grad_part(1, 1, 0)
     for dz in (1, 3, 2):
-        due(("t", 0, 0, dz))
-        cot_copy(0, (0, dz), (1, dz), tp_dev(1 - yh, z))
-    for dz in (1, 3, 2):
         grad = grad + grad_part(0, 0, dz)
-        due(("t", 1, 0, dz))
+        due(("t", 1, 0, dz, 0))
+        due(("t", 1, 0, dz, 1))
         grad = grad + grad_part(1, 0, dz)
     for a, dz in ((0, 0), (0, 1), (0, 3), (0, 2), (1, 1), (1, 3), (1, 2)):
-        due(("t", a, 1, dz))
+        due(("t", a, 1, dz, 0))
+        due(("t", a, 1, dz, 1))
         grad = grad + grad_part(a, 1, dz)
     g_tx[...] = grad.astype(BF16)
 
@@ -589,35 +610,27 @@
 
     due("tw")
 
-    def tw_view(a, dyh, dz):
+    def tw_view(dyh, dz):
         pyh = lax.rem(yh + dyh, 2)
         pz = lax.rem(z + 4 - dz, 4)
         rows = pl.ds(pl.multiple_of(80 * (pz % 2), 16), 80)
-        return tw.at[4 * a : 4 * a + 4, pz // 2, rows, lanes(pyh, HD)]
-
-    def twg_copy(a, origin, slot, dev):
-        view = tw_view(a, *origin)
-        src = tw_part.at[4 * a : 4 * a + 4] if origin == (0, 0) else view
-        sem = (a,) + slot
-        copy = remote(src, view, twg_send.at[sem], twg_recv.at[sem], dev)
-        launch(copy)
-        owed[("twg",) + sem] = copy.wait_recv
-
-    for a in range(2):
-        local_copy(tw_part.at[4 * a : 4 * a + 4], tw_view(a, 0, 0), twg_recv.at[a, 0, 0]).start()
-        owed["twg", a, 0, 0] = lambda a=a: wait_for(tw_view(a, 0, 0), twg_recv.at[a, 0, 0])
+        return tw.at[:, pz // 2, rows, lanes(pyh, HD)]
+
+    def twg_copy(origin, slot, dev):
+        view = tw_view(*origin)
+        src = tw_part if origin == (0, 0) else view
+        stage("twg", slot, src, view, twg_send, twg_recv, dev)
+
+    twg_copy((0, 0), (1, 0), tp_dev(1 - yh, z))
+    local_copy(tw_part, tw_view(0, 0), twg_recv.at[0, 0]).start()
+    owed["twg", 0, 0] = lambda: wait_for(tw_view(0, 0), twg_recv.at[0, 0])
+    for dz in far:
+        twg_copy((0, 0), (0, dz), tp_dev(yh, ring(z, dz)))
+
+    def tw_pass_on():
+        due(("twg", 1, 0))
         for dz in far:
-            twg_copy(a, (0, 0), (0, dz), tp_dev(yh, ring(z, dz)))
-    for a in (1, 0):
-        twg_copy(a, (0, 0), (1, 0), tp_dev(1 - yh, z))
-
-    def tw_pass_on():
-        due(("twg", 1, 1, 0))
-        for dz in far:
-            twg_copy(1, (1, 0), (1, dz), tp_dev(yh, ring(z, dz)))
-        for dz in (1, 3, 2):
-            due(("twg", 0, 0, dz))
-            twg_copy(0, (0, dz), (1, dz), tp_dev(1 - yh, z))
+            twg_copy((1, 0), (1, dz), tp_dev(yh, ring(z, dz)))
 
     due("g")
     gt = g[...].reshape(NQ, HD).astype(F32).T
@@ -675,12 +688,13 @@
 
         return state
 
-    lax.fori_loop(0, 8, back_step, 0)
+    lax.fori_loop(0, 5, back_step, 0)
+    tw_pass_on()
+    lax.fori_loop(5, 8, back_step, 0)
     dq_tx[...] = (dqt[...] * SCALE).T.astype(BF16).reshape(2, 2, ROWS, HD)
     to_owners(dq_tx, dq_rx.at[:, lanes(head, HD)], dq_send, dq_recv, "start")
     owed["dq"] = lambda: wait_for(dq_rx, dq_recv)
     pending.append(lambda: to_owners(dq_tx, dq_rx.at[:, lanes(head, HD)], dq_send, dq_recv, "wait"))
-    tw_pass_on()
     dkv_rx[m] = both_cores(m).astype(BF16)
 
     due("atx")
@@ -688,11 +702,10 @@
     atf = remote(at.at[:, c], at.at[:, c], atf_send, atf_recv, (sibling, t))
     launch(atf)
     owed["atf"] = atf.wait_recv
-    for a in range(2):
-        for dyh in range(2):
-            for dz in range(4):
-                if ("twg", a, dyh, dz) in owed:
-                    due(("twg", a, dyh, dz))
+    for dyh in range(2):
+        for dz in range(4):
+            if (dyh, dz) != (1, 0):
+                due(("twg", dyh, dz))
     due("atf")
 
     gw = jnp.zeros((512, 256), F32)
@@ -798,22 +811,22 @@
         dma,
         dma,
         dma,
-        dma((4,)),
-        dma((4,)),
-        dma,
-        dma,
-        dma,
-        dma,
-        dma((4,)),
-        dma((4,)),
-        dma((2, 2, 4)),
-        dma((2, 2, 4)),
+        dma((2, 4)),
+        dma((2, 4)),
+        dma((2,)),
+        dma((2,)),
+        dma((2,)),
+        dma((2,)),
+        dma((2, 4)),
+        dma((2, 4)),
+        dma((2, 2, 4, 2)),
+        dma((2, 2, 4, 2)),
         dma((1, 4)),
         dma,
         dma((16,)),
         dma,
-        dma((2, 2, 4)),
-        dma((2, 2, 4)),
+        dma((2, 4)),
+        dma((2, 4)),
         dma((2, 2)),
         dma,
         dma((8,)),

time: 106 us -> 94.5 us (0.89)
  Pallas kernels: 105 us -> 92.6 us
    pallas_call x1, Pallas kernels: 103 us -> 90.3 us  [on_device(): pl.pallas_call(kernel, out_shape=(jax.ShapeDtypeStruct((ROWS, 512), BF16)...]
where the time goes in v4:
time: 94.5 us; the launch traced here: 93.2 us
  Pallas kernels  92.6 us (98%)
    pallas_call x1, Pallas kernels, on_device(): pl.pallas_call(kernel, out_shape=(jax.ShapeDtypeStruct((ROWS, 512), BF16)...  90.3 us
    pallas_call x1, Pallas kernels, on_device(): pl.pallas_call(scaled, out_shape=tuple((jax.ShapeDtypeStruct(part.shape,...  2.27 us

profile of v4, /device:TPU:1, one launch (start us, length us, event | category | flops | bytes accessed | tf_op | source)
XLA Modules:
  0.0 93.2 jit_solution(10890126826729753073)
XLA Ops:
  0.6 90.3 %shard_map.138 = (bf16[160,512]{1,0:T(8,128)(2,1)}, f32[160,512]{1,0:T(8,128)}, f32[160,512]{1,0:T(8,128)}, f32[512,256]{1,0:T(8,128)}, f32[8,128]{1,0:T(8,128)}) custom-call(s32[16]{0:T(128)} %frame_ref.1, s32[16]{0:T(128)} %time_ref.1, bf16[160,512]{1,0:T(8,128)(2,1)} %q_ref.1, bf16[160,512]{1,0:T(8,128)(2,1)} %k_ref.1, bf16[160,512]{1,0:T(8,128)(2,1)} %v_ref.1, ...), custom_call_target="tpu_custom_call" | custom-call | flops 7000000000 | bytes 8000000 | tf_op jit(solution)/shard_map/pallas_call | solution.py:841
  90.9 2.3 %shard_map.139 = (bf16[160,512]{1,0:T(8,128)(2,1)}, bf16[160,512]{1,0:T(8,128)(2,1)}, bf16[160,512]{1,0:T(8,128)(2,1)}, bf16[512,256]{1,0:T(8,128)(2,1)}) custom-call(f32[8,128]{1,0:T(8,128)} %get-tuple-element.9.ms_ref, bf16[160,512]{1,0:T(8,128)(2,1)} %get-tuple-element.10.refs_0_, f32[160,512]{1,0:T(8,128)} %get-tuple-element.11.refs_1_, ...), custom_call_target="tpu_custom_call" | custom-call | tf_op jit(solution)/shard_map/pallas_call | solution.py:858

commit v5 on v4

--- a/solution.py
+++ b/solution.py
@@ -63,6 +63,8 @@
     at_own,
     at,
     negb,
+    lat,
+    lat_sem,
     part_a,
     part_b,
     rx_a,
@@ -120,6 +122,8 @@
     g_send,
     g_recv,
     tw_send,
+    twd_send,
+    twd_recv,
     tw_recv,
     twg_send,
     twg_recv,
@@ -187,6 +191,10 @@
 
     wload = pltpu.make_async_copy(w_hbm, w, wsem)
     wload.start()
+    lat_loads = [pltpu.make_async_copy(ref, lat.at[i], lat_sem.at[i]) for i, ref in enumerate((noisy_ref, vel_ref))]
+    for i, load in enumerate(lat_loads):
+        load.start()
+        owed["lat", i] = load.wait
     owed["w"] = wload.wait
 
     barrier = pltpu.get_barrier_semaphore()
@@ -289,13 +297,14 @@
                     def _():
                         local_copy(src.at[u, core], dst, recv).start()
 
-    def q_moves(act):
-        for a, ref in ((1, q_ref), (0, qd_ref)):
+    def q_moves(act, which=(1, 0)):
+        for a in which:
+            ref = (qd_ref, q_ref)[a]
             to_heads(
                 lambda hx, ref=ref: ref.at[:, lanes(hx, HD)],
                 qq.at[unit, c, :, a * HD : (a + 1) * HD],
                 q_send,
-                q_recv,
+                q_recv.at[a],
                 a,
                 act,
             )
@@ -304,10 +313,12 @@
     for a in range(4):
         kv_own(a)
     kv_along_x(1)
+    q_moves("start", (1,))
     kv_along_x(2)
-    q_moves("start")
+    q_moves("start", (0,))
     pending.append(lambda: q_moves("wait"))
-    owed["q"] = lambda: wait_for(qq, q_recv)
+    for a in range(2):
+        owed["q", a] = lambda a=a: wait_for(qq.at[:, :, :, a * HD : (a + 1) * HD], q_recv.at[a])
     kv_along_x(3)
 
     ends = []
@@ -335,8 +346,10 @@
 
     rpos = s * ROWS + t * 20 + lax.broadcasted_iota(jnp.int32, (20, 1), 0)
     _, cosr, sinr = frame_facts(rpos)
+    for i in range(2):
+        due(("lat", i))
     negb[...] = jnp.zeros_like(negb)
-    negb[0:20, :] = sinr * cosr * noisy_ref[...].astype(F32) - cosr * cosr * vel_ref[...].astype(F32)
+    negb[0:20, :] = sinr * cosr * lat[0].astype(F32) - cosr * cosr * lat[1].astype(F32)
 
     n0 = chip0 + 2
     n1 = jnp.minimum(chip1 + 2, 8)
@@ -356,8 +369,7 @@
     kv_across(1)
     kv_across(2)
     kv_received(0)
-    kv_received(1)
-    due("q")
+    due(("q", 1))
     kv_complete(0)
 
     def chunk(buf, i):
@@ -365,7 +377,7 @@
 
     def pass1(i, top, lo):
         keys = kk[i // 2, i % 2, :, :, :HD].reshape(UNIT, HD)
-        queries = qq[...].reshape(NQ, 2 * HD)[lo:, HD:]
+        queries = qq[:, :, :, HD:].reshape(NQ, HD)[lo:]
         sc = dot_nt(keys, queries) * SCALE
         kpos = i * UNIT + lax.broadcasted_iota(jnp.int32, (UNIT, 1), 0)
         sc = jnp.where(kpos < kend[:, lo:], sc, -1e30)
@@ -374,6 +386,8 @@
 
     top = over_keys(pass1, jnp.full((1, NQ), -1e30, F32))
 
+    kv_received(1)
+    due(("q", 0))
     kv_across(3)
     kv_complete(1)
 
@@ -393,30 +407,27 @@
     mean = tan * inv
     kv_complete(2)
 
-    acc1[...] = jnp.zeros_like(acc1)
     acc2[...] = jnp.zeros_like(acc2)
 
     def pass3(i, state, lo):
         p = sbuf[i, :, lo:] * inv[:, lo:]
-        ph = p.astype(BF16)
-        p16[i, :, lo:] = ph
+        p16[i, :, lo:] = p.astype(BF16)
         ds = (p * (stbuf[i, :, lo:] - mean[:, lo:])).astype(BF16)
         vals = vv[i // 2, i % 2, :, :, :HD].reshape(UNIT, HD)
-        acc1[:, lo:] += dot_tn(vals, ph)
         acc2[:, lo:] += dot_tn(vals, ds)
         return state
 
     over_keys(pass3, 0, lambda: kv_received(3))
     kv_complete(3)
+    acc1[...] = jnp.zeros_like(acc1)
 
     def pass4(i, state, lo):
-        vals_dot = vv[i // 2, i % 2, :, :, HD:].reshape(UNIT, HD)
-        acc2[:, lo:] += dot_tn(vals_dot, p16[i, :, lo:])
+        acc1[:, lo:] += dot_tn(chunk(vv, i), p16[i, :, lo:])
         return state
 
     over_keys(pass4, 0)
-    attn_t = acc1[...].astype(BF16)
-    tan_t = acc2[...].astype(BF16)
+    attn_t = acc1[0:HD].astype(BF16)
+    tan_t = (acc2[...] + acc1[HD:]).astype(BF16)
     at_own[...] = attn_t
     u_t = (0.5 * cosq) * (cosq * attn_t.astype(F32) + sinq * tan_t.astype(F32))
     ublk[...] = u_t.T.astype(BF16).reshape(2, 2, ROWS, HD)
@@ -426,6 +437,9 @@
 
     def at_view(py, hx):
         return at.at[py, c, lanes(hx, HD), :]
+
+    launch(remote(at_own, at_view(y, x), aty_send, aty_recv, seq_dev(x, 1 - y, c)))
+    owed["aty"] = lambda: wait_for(at_view(1 - y, x), aty_recv)
 
     def at_pass_on():
         due("aty")
@@ -477,8 +491,6 @@
     send_a(1)
 
     local_copy(at_own, at_view(y, x), atx_recv).start()
-    launch(remote(at_own, at_view(y, x), aty_send, aty_recv, seq_dev(x, 1 - y, c)))
-    owed["aty"] = lambda: wait_for(at_view(1 - y, x), aty_recv)
     for dx in far:
         launch(remote(at_own, at_view(y, x), atx_send.at[0, dx], atx_recv, seq_dev(ring(x, dx), y, c)))
     owed["atx"] = lambda: wait_for(at.at[y, c], atx_recv)
@@ -577,19 +589,24 @@
     row_half = pl.ds(pl.multiple_of(80 * (z % 2), 16), 80)
     chip_slot = y * 4 + home * 2 + unit
 
+    def tw_source(dest):
+        tt = dest // 2
+        dyh = lax.rem(yh + tt // 4, 2)
+        dz = lax.rem(z + 4 - tt % 4, 4)
+        return cot.at[dest % 2, dyh, dz]
+
     def tw_send_all(act):
-        for d in (8, 9, 7, 6, 10, 4, 12, 5, 11, 3, 13, 2, 14, 1, 15, 0):
-            dest = lax.rem(s + d, 16)
-            tt = dest // 2
-            dyh = lax.rem(yh + tt // 4, 2)
-            dz = lax.rem(z + 4 - tt % 4, 4)
-            src = cot.at[dest % 2, dyh, dz, row_half, lanes(yh, HD)]
-            dst = tw_part.at[chip_slot]
-            if d:
-                copy = remote(src, dst, tw_send.at[d], tw_recv, (dest, t))
+        for dx in (2, 1, 3, 0):
+            for pc in range(2):
+                dest, _ = seq_dev(ring(x, dx), 1 - y, pc)
+                copy = remote(
+                    tw_source(dest).at[row_half, lanes(yh, HD)],
+                    tw_part.at[home * 2 + unit],
+                    tw_send.at[dx, pc],
+                    tw_recv,
+                    (dest, t),
+                )
                 copy.start() if act == "start" else copy.wait_send()
-            elif act == "start":
-                local_copy(src, dst, tw_recv).start()
 
     def tw_turn(act):
         @pl.when(c == z // 2)
@@ -597,16 +614,16 @@
             tw_send_all(act)
 
     tw_turn("start")
+    for dx in (2, 1, 3, 0):
+        for e in range(2):
+            dest, _ = seq_dev(ring(x, dx), y, c if e == 0 else 1 - c)
+            if dx or e:
+                launch(remote(tw_source(dest), tw.at[chip_slot, c], twd_send.at[dx, e], twd_recv, (dest, t)))
+            else:
+                local_copy(tw_source(s), tw.at[chip_slot, c], twd_recv).start()
+    owed["twd"] = lambda: wait_for(tw.at[pl.ds(y * 4, 4)], twd_recv)
     owed["tw"] = lambda: wait_for(tw_part, tw_recv)
     pending.append(lambda: tw_turn("wait"))
-
-    sqv = sq_tp[0]
-    for d in range(1, 8):
-        due(("sqt", d))
-        sqv = sqv + sq_tp[d]
-    sq_seq[0] = sqv
-    for d in range(1, 16):
-        sq_copy(sq_seq, d, sqs_send, sqs_recv, (lax.rem(s + d, 16), t), "sqs")
 
     due("tw")
 
@@ -614,7 +631,7 @@
         pyh = lax.rem(yh + dyh, 2)
         pz = lax.rem(z + 4 - dz, 4)
         rows = pl.ds(pl.multiple_of(80 * (pz % 2), 16), 80)
-        return tw.at[:, pz // 2, rows, lanes(pyh, HD)]
+        return tw.at[pl.ds((1 - y) * 4, 4), pz // 2, rows, lanes(pyh, HD)]
 
     def twg_copy(origin, slot, dev):
         view = tw_view(*origin)
@@ -690,6 +707,14 @@
 
     lax.fori_loop(0, 5, back_step, 0)
     tw_pass_on()
+    sqv = sq_tp[0]
+    for d in range(1, 8):
+        due(("sqt", d))
+        sqv = sqv + sq_tp[d]
+    sq_seq[0] = sqv
+    for d in range(1, 16):
+        sq_copy(sq_seq, d, sqs_send, sqs_recv, (lax.rem(s + d, 16), t), "sqs")
+
     lax.fori_loop(5, 8, back_step, 0)
     dq_tx[...] = (dqt[...] * SCALE).T.astype(BF16).reshape(2, 2, ROWS, HD)
     to_owners(dq_tx, dq_rx.at[:, lanes(head, HD)], dq_send, dq_recv, "start")
@@ -706,6 +731,7 @@
         for dz in range(4):
             if (dyh, dz) != (1, 0):
                 due(("twg", dyh, dz))
+    due("twd")
     due("atf")
 
     gw = jnp.zeros((512, 256), F32)
@@ -760,13 +786,15 @@
         pltpu.VMEM((8, UNIT, NQ), F32),
         pltpu.VMEM((8, UNIT, NQ), F32),
         pltpu.VMEM((8, UNIT, NQ), BF16),
-        pltpu.VMEM((HD, NQ), F32),
+        pltpu.VMEM((2 * HD, NQ), F32),
         pltpu.VMEM((HD, NQ), F32),
         pltpu.VMEM((2, 2, ROWS, HD), BF16),
         pltpu.VMEM((ROWS, 512), BF16),
         pltpu.VMEM((HD, NQ), BF16),
         pltpu.VMEM((2, 2, 512, NQ), BF16),
         pltpu.VMEM((32, 4096), F32),
+        pltpu.VMEM((2, 20, 4096), BF16),
+        dma((2,)),
         pltpu.VMEM((4, 2, ROWS, 256), BF16),
         pltpu.VMEM((4, ROWS, 256), BF16),
         pltpu.VMEM((4, 2, ROWS, 256), BF16),
@@ -787,7 +815,7 @@
         pltpu.VMEM((2, 8, ROWS, HD), BF16),
         pltpu.VMEM((2, 8, ROWS, HD), BF16),
         pltpu.VMEM((8, 2, ROWS, HD), BF16),
-        pltpu.VMEM((8, 80, HD), BF16),
+        pltpu.VMEM((4, 80, HD), BF16),
         pltpu.VMEM((8, 2, ROWS, 256), BF16),
         pltpu.VMEM((8, 8, 128), F32),
         pltpu.VMEM((16, 8, 128), F32),
@@ -801,7 +829,7 @@
         dma((4,)),
         dma((4,)),
         dma((2, 4)),
-        dma,
+        dma((2,)),
         dma((2, 2)),
         dma,
         dma((2, 4)),
@@ -823,7 +851,9 @@
         dma((2, 2, 4, 2)),
         dma((1, 4)),
         dma,
-        dma((16,)),
+        dma((4, 2)),
+        dma((4, 2)),
+        dma,
         dma,
         dma((2, 4)),
         dma((2, 4)),
@@ -847,7 +877,7 @@
             jax.ShapeDtypeStruct((512, 256), F32),
             jax.ShapeDtypeStruct((8, 128), F32),
         ),
-        in_specs=[smem, smem] + [hbm] * 7 + [vmem] * 2,
+        in_specs=[smem, smem] + [hbm] * 9,
         out_specs=(vmem,) * 5,
         scratch_shapes=scratch,
         compiler_params=pltpu.CompilerParams(

time: 94.5 us -> 90.3 us (0.956); the launches traced: 93.2 us -> 90.2 us
  Pallas kernels: 92.6 us -> 89.5 us
    pallas_call x1, Pallas kernels: 90.3 us -> 87.3 us  [on_device(): pl.pallas_call(kernel, out_shape=(jax.ShapeDtypeStruct((ROWS, 512), BF16)...]
where the time goes in v5:
time: 90.3 us; the launch traced here: 90.2 us
  Pallas kernels  89.5 us (99%)
    pallas_call x1, Pallas kernels, on_device(): pl.pallas_call(kernel, out_shape=(jax.ShapeDtypeStruct((ROWS, 512), BF16)...  87.3 us
    pallas_call x1, Pallas kernels, on_device(): pl.pallas_call(scaled, out_shape=tuple((jax.ShapeDtypeStruct(part.shape,...  2.27 us

profile of v5, /device:TPU:1, one launch (start us, length us, event | category | flops | bytes accessed | tf_op | source)
XLA Modules:
  0.0 90.2 jit_solution(3585510381193903760)
XLA Ops:
  0.6 87.3 %shard_map.138 = (bf16[160,512]{1,0:T(8,128)(2,1)}, f32[160,512]{1,0:T(8,128)}, f32[160,512]{1,0:T(8,128)}, f32[512,256]{1,0:T(8,128)}, f32[8,128]{1,0:T(8,128)}) custom-call(s32[16]{0:T(128)} %frame_ref.1, s32[16]{0:T(128)} %time_ref.1, bf16[160,512]{1,0:T(8,128)(2,1)} %q_ref.1, bf16[160,512]{1,0:T(8,128)(2,1)} %k_ref.1, bf16[160,512]{1,0:T(8,128)(2,1)} %v_ref.1, ...), custom_call_target="tpu_custom_call" | custom-call | flops 7000000000 | bytes 8000000 | tf_op jit(solution)/shard_map/pallas_call | solution.py:871
  87.9 2.3 %shard_map.139 = (bf16[160,512]{1,0:T(8,128)(2,1)}, bf16[160,512]{1,0:T(8,128)(2,1)}, bf16[160,512]{1,0:T(8,128)(2,1)}, bf16[512,256]{1,0:T(8,128)(2,1)}) custom-call(f32[8,128]{1,0:T(8,128)} %get-tuple-element.9.ms_ref, bf16[160,512]{1,0:T(8,128)(2,1)} %get-tuple-element.10.refs_0_, f32[160,512]{1,0:T(8,128)} %get-tuple-element.11.refs_1_, ...), custom_call_target="tpu_custom_call" | custom-call | tf_op jit(solution)/shard_map/pallas_call | solution.py:888

commit v6 on v5

--- a/solution.py
+++ b/solution.py
@@ -14,6 +14,7 @@
 UNIT = 320
 NCHIP = 8
 NQ = 640
+CUTS = (0, 80, 160)
 SCALE = 1.0 / math.sqrt(HD)
 MESH = pl.DeviceIdType.MESH
 F32 = jnp.float32
@@ -463,7 +464,8 @@
 
     for dz in range(4):
         part_b[dz] = partial(1 - yh, ring(z, dz), 1).astype(BF16)
-    halves = [slice(0, 80), slice(80, 160)]
+    halves = [slice(lo, hi) for lo, hi in zip(CUTS[:-1], CUTS[1:])]
+    pieces = range(len(halves))
 
     def stage(name, key, src, dst, send, recv, dev):
         copy = remote(src, dst, send.at[key], recv.at[key], dev)
@@ -487,14 +489,17 @@
             stage("rsa", (hf, dz), part_a.at[dz, :, rows], rx_a.at[dz, :, rows], rsa_send, rsa_recv, dev)
 
     send_a(0)
-    send_b(1)
-    send_a(1)
+    for hf in pieces[1:]:
+        send_b(hf)
+        send_a(hf)
 
     local_copy(at_own, at_view(y, x), atx_recv).start()
     for dx in far:
         launch(remote(at_own, at_view(y, x), atx_send.at[0, dx], atx_recv, seq_dev(ring(x, dx), y, c)))
     owed["atx"] = lambda: wait_for(at.at[y, c], atx_recv)
 
+    at_pass_on()
+
     for dz in range(4):
         sum_b[dz] = partial(yh, ring(z, dz), 1)
     for e in range(2):
@@ -506,7 +511,7 @@
         sem = (a,) + dst + (hf,)
         stage("t", sem, cot.at[(a,) + src + (rows,)], cot.at[(a,) + dst + (rows,)], t_send, t_recv, dev)
 
-    for hf in range(2):
+    for hf in pieces:
         rows = halves[hf]
         due(("rsb", hf))
         for dz in far:
@@ -521,7 +526,7 @@
         stage("rsa2", (hf,), part_a2.at[rows], rx_a2.at[rows], rsa2_send, rsa2_recv, tp_dev(1 - yh, z))
 
     sq = jnp.zeros((1, 256), F32)
-    for hf in range(2):
+    for hf in pieces:
         rows = halves[hf]
         cot_a = sum_a[0, rows]
         for dz in far:
@@ -551,8 +556,6 @@
     for d in range(1, 8):
         sq_copy(sq_tp, d, sqt_send, sqt_recv, (s, lax.rem(t + d, 8)), "sqt")
 
-    at_pass_on()
-
     def grad_part(a, dyh, dz):
         pyh = lax.rem(yh + dyh, 2)
         pz = lax.rem(z + 4 - dz, 4)
@@ -560,7 +563,7 @@
         return dot_nt(cot[a, dyh, dz], w[:, cols])
 
     grad = grad_part(0, 0, 0) + grad_part(1, 0, 0)
-    for hf in range(2):
+    for hf in pieces:
         due(("t", 1, 1, 0, hf))
         for dz in far:
             cot_copy(1, (1, 0), (1, dz), tp_dev(yh, ring(z, dz)), hf)
@@ -570,12 +573,12 @@
     grad = grad + grad_part(1, 1, 0)
     for dz in (1, 3, 2):
         grad = grad + grad_part(0, 0, dz)
-        due(("t", 1, 0, dz, 0))
-        due(("t", 1, 0, dz, 1))
+        for hf in pieces:
+            due(("t", 1, 0, dz, hf))
         grad = grad + grad_part(1, 0, dz)
     for a, dz in ((0, 0), (0, 1), (0, 3), (0, 2), (1, 1), (1, 3), (1, 2)):
-        due(("t", a, 1, dz, 0))
-        due(("t", a, 1, dz, 1))
+        for hf in pieces:
+            due(("t", a, 1, dz, hf))
         grad = grad + grad_part(a, 1, dz)
     g_tx[...] = grad.astype(BF16)
 
@@ -625,8 +628,6 @@
     owed["tw"] = lambda: wait_for(tw_part, tw_recv)
     pending.append(lambda: tw_turn("wait"))
 
-    due("tw")
-
     def tw_view(dyh, dz):
         pyh = lax.rem(yh + dyh, 2)
         pz = lax.rem(z + 4 - dz, 4)
@@ -638,11 +639,13 @@
         src = tw_part if origin == (0, 0) else view
         stage("twg", slot, src, view, twg_send, twg_recv, dev)
 
-    twg_copy((0, 0), (1, 0), tp_dev(1 - yh, z))
-    local_copy(tw_part, tw_view(0, 0), twg_recv.at[0, 0]).start()
-    owed["twg", 0, 0] = lambda: wait_for(tw_view(0, 0), twg_recv.at[0, 0])
-    for dz in far:
-        twg_copy((0, 0), (0, dz), tp_dev(yh, ring(z, dz)))
+    def tw_spread():
+        due("tw")
+        twg_copy((0, 0), (1, 0), tp_dev(1 - yh, z))
+        local_copy(tw_part, tw_view(0, 0), twg_recv.at[0, 0]).start()
+        owed["twg", 0, 0] = lambda: wait_for(tw_view(0, 0), twg_recv.at[0, 0])
+        for dz in far:
+            twg_copy((0, 0), (0, dz), tp_dev(yh, ring(z, dz)))
 
     def tw_pass_on():
         due(("twg", 1, 0))
@@ -680,6 +683,10 @@
         sib_copy(i).wait_recv()
         return dkv[:, i, c].astype(F32) + sib_rx[:, i].astype(F32)
 
+    def pass_to_owner(i):
+        dkv_tx[:, i] = both_cores(i).astype(BF16)
+        dkv_copy(i).start()
+
     def back_step(k, state):
         i = lax.rem(m + 1 + k, 8)
 
@@ -699,14 +706,19 @@
 
         @pl.when(k > 0)
         def _():
-            done = lax.rem(m + k, 8)
-            dkv_tx[:, done] = both_cores(done).astype(BF16)
-            dkv_copy(done).start()
+            pass_to_owner(lax.rem(m + k, 8))
 
         return state
 
-    lax.fori_loop(0, 5, back_step, 0)
+    lax.fori_loop(0, 1, back_step, 0)
+    tw_spread()
+    lax.fori_loop(1, 6, back_step, 0)
     tw_pass_on()
+    due("atx")
+    due("at2")
+    atf = remote(at.at[:, c], at.at[:, c], atf_send, atf_recv, (sibling, t))
+    launch(atf)
+    owed["atf"] = atf.wait_recv
     sqv = sq_tp[0]
     for d in range(1, 8):
         due(("sqt", d))
@@ -715,18 +727,13 @@
     for d in range(1, 16):
         sq_copy(sq_seq, d, sqs_send, sqs_recv, (lax.rem(s + d, 16), t), "sqs")
 
-    lax.fori_loop(5, 8, back_step, 0)
+    lax.fori_loop(6, 8, back_step, 0)
     dq_tx[...] = (dqt[...] * SCALE).T.astype(BF16).reshape(2, 2, ROWS, HD)
     to_owners(dq_tx, dq_rx.at[:, lanes(head, HD)], dq_send, dq_recv, "start")
     owed["dq"] = lambda: wait_for(dq_rx, dq_recv)
     pending.append(lambda: to_owners(dq_tx, dq_rx.at[:, lanes(head, HD)], dq_send, dq_recv, "wait"))
     dkv_rx[m] = both_cores(m).astype(BF16)
 
-    due("atx")
-    due("at2")
-    atf = remote(at.at[:, c], at.at[:, c], atf_send, atf_recv, (sibling, t))
-    launch(atf)
-    owed["atf"] = atf.wait_recv
     for dyh in range(2):
         for dz in range(4):
             if (dyh, dz) != (1, 0):
@@ -839,16 +846,16 @@
         dma,
         dma,
         dma,
-        dma((2, 4)),
-        dma((2, 4)),
-        dma((2,)),
-        dma((2,)),
-        dma((2,)),
-        dma((2,)),
-        dma((2, 4)),
-        dma((2, 4)),
-        dma((2, 2, 4, 2)),
-        dma((2, 2, 4, 2)),
+        dma((len(CUTS) - 1, 4)),
+        dma((len(CUTS) - 1, 4)),
+        dma((len(CUTS) - 1,)),
+        dma((len(CUTS) - 1,)),
+        dma((len(CUTS) - 1,)),
+        dma((len(CUTS) - 1,)),
+        dma((len(CUTS) - 1, 4)),
+        dma((len(CUTS) - 1, 4)),
+        dma((2, 2, 4, len(CUTS) - 1)),
+        dma((2, 2, 4, len(CUTS) - 1)),
         dma((1, 4)),
         dma,
         dma((4, 2)),

time: 90.3 us -> 89.5 us (level)
  no operation moved by 1% of the time
where the time goes in v6:
time: 89.5 us; the launch traced here: 89.3 us
  Pallas kernels  88.7 us (99%)
    pallas_call x1, Pallas kernels, on_device(): pl.pallas_call(kernel, out_shape=(jax.ShapeDtypeStruct((ROWS, 512), BF16)...  86.4 us
    pallas_call x1, Pallas kernels, on_device(): pl.pallas_call(scaled, out_shape=tuple((jax.ShapeDtypeStruct(part.shape,...  2.27 us

profile of v6, /device:TPU:1, one launch (start us, length us, event | category | flops | bytes accessed | tf_op | source)
XLA Modules:
  0.0 89.3 jit_solution(4208716693239087555)
XLA Ops:
  0.6 86.4 %shard_map.138 = (bf16[160,512]{1,0:T(8,128)(2,1)}, f32[160,512]{1,0:T(8,128)}, f32[160,512]{1,0:T(8,128)}, f32[512,256]{1,0:T(8,128)}, f32[8,128]{1,0:T(8,128)}) custom-call(s32[16]{0:T(128)} %frame_ref.1, s32[16]{0:T(128)} %time_ref.1, bf16[160,512]{1,0:T(8,128)(2,1)} %q_ref.1, bf16[160,512]{1,0:T(8,128)(2,1)} %k_ref.1, bf16[160,512]{1,0:T(8,128)(2,1)} %v_ref.1, ...), custom_call_target="tpu_custom_call" | custom-call | flops 7000000000 | bytes 8000000 | tf_op jit(solution)/shard_map/pallas_call | solution.py:878
  87.1 2.3 %shard_map.139 = (bf16[160,512]{1,0:T(8,128)(2,1)}, bf16[160,512]{1,0:T(8,128)(2,1)}, bf16[160,512]{1,0:T(8,128)(2,1)}, bf16[512,256]{1,0:T(8,128)(2,1)}) custom-call(f32[8,128]{1,0:T(8,128)} %get-tuple-element.9.ms_ref, bf16[160,512]{1,0:T(8,128)(2,1)} %get-tuple-element.10.refs_0_, f32[160,512]{1,0:T(8,128)} %get-tuple-element.11.refs_1_, ...), custom_call_target="tpu_custom_call" | custom-call | tf_op jit(solution)/shard_map/pallas_call | solution.py:895

commit v7 on v6

--- a/solution.py
+++ b/solution.py
@@ -734,17 +734,21 @@
     pending.append(lambda: to_owners(dq_tx, dq_rx.at[:, lanes(head, HD)], dq_send, dq_recv, "wait"))
     dkv_rx[m] = both_cores(m).astype(BF16)
 
+    def weight_part(py):
+        out = jnp.zeros((512, 256), F32)
+        for e in range(2):
+            rows = tw[pl.ds(py * 4 + 2 * e, 2)].reshape(NQ, 256)
+            out = out + dot_nn(at[py, e], rows)
+        return out
+
+    due("twd")
+    due("atf")
+    gw = weight_part(y)
     for dyh in range(2):
         for dz in range(4):
             if (dyh, dz) != (1, 0):
                 due(("twg", dyh, dz))
-    due("twd")
-    due("atf")
-
-    gw = jnp.zeros((512, 256), F32)
-    for a in range(4):
-        rows = tw[2 * a : 2 * a + 2].reshape(NQ, 256)
-        gw = gw + dot_nn(at[a // 2, a % 2], rows)
+    gw = gw + weight_part(1 - y)
     gw_out[...] = gw
 
     sqv = sq_seq[0]

time: 89.5 us -> 89.5 us (level)
  no operation moved by 1% of the time
where the time goes in v7:
time: 89.5 us; the launch traced here: 89.3 us
  Pallas kernels  88.7 us (99%)
    pallas_call x1, Pallas kernels, on_device(): pl.pallas_call(kernel, out_shape=(jax.ShapeDtypeStruct((ROWS, 512), BF16)...  86.4 us
    pallas_call x1, Pallas kernels, on_device(): pl.pallas_call(scaled, out_shape=tuple((jax.ShapeDtypeStruct(part.shape,...  2.27 us

profile of v7, /device:TPU:1, one launch (start us, length us, event | category | flops | bytes accessed | tf_op | source)
XLA Modules:
  0.0 89.3 jit_solution(3876522834770557963)
XLA Ops:
  0.6 86.4 %shard_map.138 = (bf16[160,512]{1,0:T(8,128)(2,1)}, f32[160,512]{1,0:T(8,128)}, f32[160,512]{1,0:T(8,128)}, f32[512,256]{1,0:T(8,128)}, f32[8,128]{1,0:T(8,128)}) custom-call(s32[16]{0:T(128)} %frame_ref.1, s32[16]{0:T(128)} %time_ref.1, bf16[160,512]{1,0:T(8,128)(2,1)} %q_ref.1, bf16[160,512]{1,0:T(8,128)(2,1)} %k_ref.1, bf16[160,512]{1,0:T(8,128)(2,1)} %v_ref.1, ...), custom_call_target="tpu_custom_call" | custom-call | flops 7000000000 | bytes 8000000 | tf_op jit(solution)/shard_map/pallas_call | solution.py:882
  87.1 2.3 %shard_map.139 = (bf16[160,512]{1,0:T(8,128)(2,1)}, bf16[160,512]{1,0:T(8,128)(2,1)}, bf16[160,512]{1,0:T(8,128)(2,1)}, bf16[512,256]{1,0:T(8,128)(2,1)}) custom-call(f32[8,128]{1,0:T(8,128)} %get-tuple-element.9.ms_ref, bf16[160,512]{1,0:T(8,128)(2,1)} %get-tuple-element.10.refs_0_, f32[160,512]{1,0:T(8,128)} %get-tuple-element.11.refs_1_, ...), custom_call_target="tpu_custom_call" | custom-call | tf_op jit(solution)/shard_map/pallas_call | solution.py:899
